TPU v7x, 256 devices: a whole 4x4x8 slice. The times are simulated.
256 devices in a mesh: gz: 8 (over x, core), xy: 32 (over y, z).
Axes of the slice: x: 4, y: 4, z: 8, core: 2. Of those that a mesh axis runs over, the one named last changes fastest.
Arguments:
- residual: float32 [512, 32, 1024], P('xy', None, 'gz'), may hold values from -6 to 6
- eigen_vectors: float32 [3, 10, 10], replicated, may hold values from -2 to 2
- eigen_values: float32 [3, 10], replicated, may hold values from 0.2 to 5
- element_scale: float32 [64, 4, 128], P('xy', None, 'gz'), may hold values from 0.5 to 4
- vertex_map: int32 [64, 4, 128], P('xy', None, 'gz'), may hold values from 0 to 511
- leaf_columns: float32 [131072, 512], P(('gz', 'xy')), may hold values from -0.25 to 0.25
- separator_columns: float32 [131072, 3072], P(('gz', 'xy')), may hold values from -0.25 to 0.25
- separator_mask: int32 [256, 6], P(('gz', 'xy')), may hold values 0 or 1
Outputs:
- preconditioned: float32 [512, 32, 1024], P('xy', None, 'gz')
- coarse_solution: float32 [131072], P(('gz', 'xy'))
Inputs may be any that keep to these rules, and one draw needn't show every extreme that they name: vertex_map names a vertex of the element's own device.
All inputs are finite; a program needn't handle non-finite values. No bound on the sum of `separator_mask` on one device may be relied on, other than what follows from the above.
Results may differ from a plain program's by a relative error of at most 0.0001.
Values sent between devices are 32-bit elements; how exact they have to be, the bound alone decides.
No kernel may reach another device: no remote copies, remote signals or barrier semaphores. Data moves between devices by JAX's collectives and lax.ppermute only.
A program may use at most 128 MiB of HBM per device.

v0:
```python
import functools

import jax
import jax.numpy as jnp
from jax import lax
from jax.experimental import pallas as pl
from jax.experimental.pallas import tpu as pltpu
from jax.sharding import PartitionSpec as P

NP = 8
LEVELS = 6
EX, EY, EZ = 2, 4, 16
VERTS = 512
SW = 512
ELEMS = EX * EY * EZ
NX, NY, NZ = EX * NP, EY * NP, EZ * NP
PTS = NP + 2
CHUNKS = 8
ROWS = VERTS // CHUNKS

F32 = jnp.float32
BF16 = jnp.bfloat16
HIGH = lax.Precision.HIGHEST
VMEM = pl.BlockSpec(memory_space=pltpu.VMEM)
SMEM = pl.BlockSpec(memory_space=pltpu.SMEM)
ANY = pl.BlockSpec(memory_space=pl.ANY)
FIRST_LIMIT = 40 * 2**20
PARAMS = pltpu.CompilerParams(vmem_limit_bytes=40 * 1024 * 1024)
NN = (((1,), (0,)), ((), ()))
NT = (((1,), (1,)), ((), ()))


def dot(a, b, dims=NN):
    return lax.dot_general(a, b, dims, precision=HIGH, preferred_element_type=F32)


def bdot(a, b, dims=NN):
    return lax.dot_general(a, b, dims, preferred_element_type=F32)


def split(a):
    hi = a.astype(BF16)
    return hi, (a - hi.astype(F32)).astype(BF16)


def dot3(a, b, dims=NN):
    return bdot(a[0], b[0], dims) + (bdot(a[0], b[1], dims) + bdot(a[1], b[0], dims))


def iota(shape, axis):
    return lax.broadcasted_iota(jnp.int32, shape, axis)


def div_mod(values, by):
    quotient = jnp.floor((values.astype(F32) + 0.5) * (1.0 / by)).astype(jnp.int32)
    return quotient, values - quotient * by


def mark(condition):
    return condition.astype(F32)


def split3(a):
    hi = a.astype(BF16).astype(F32)
    rest = a - hi
    mid = rest.astype(BF16).astype(F32)
    return hi, mid, rest - mid


def dot_onehot(a, onehot):
    parts = jnp.concatenate([*split3(a), jnp.zeros_like(a)], axis=0).astype(BF16)
    out = bdot(parts, onehot.astype(BF16))
    return out[0:8] + (out[8:16] + out[16:24])


def odd(axis):
    return lax.rem(lax.axis_index(axis), 2)


def factor(level):
    group = 256 if level == LEVELS - 1 else 2 ** (level + 1)
    return float(group) ** (-0.25)


def vertex_values(vm_row, row):
    out = []
    for g in range(VERTS // 8):
        vertex = (iota((8, ELEMS), 0) + g * 8).astype(F32)
        out.append(jnp.sum(jnp.where(vertex == vm_row, row, 0.0), axis=1, keepdims=True))
    return out


TILES = SW // 128
FACE = NY + 8
PARTIALS = LEVELS * TILES
LAST = PARTIALS - TILES


def first_kernel(
    r_hbm, vm_hbm, mask_hbm, q_hbm, vec_hbm, lam_hbm, scale_hbm,
    face_a_ref, face_b_ref, out_ref, aux_ref, r_ref, q_ref, vec_ref, lam_ref, scale_ref,
    v_ref, m_ref, b_ref, sem,
):
    moves = (
        (r_hbm, r_ref), (vm_hbm, v_ref), (mask_hbm, m_ref),
        (vec_hbm, vec_ref), (lam_hbm, lam_ref), (scale_hbm, scale_ref),
    )
    small = [
        pltpu.make_async_copy(src, dst, sem.at[CHUNKS + i]) for i, (src, dst) in enumerate(moves)
    ]
    for copy in small:
        copy.start()
    large = []
    for c in range(CHUNKS):
        rows = pl.ds(c * ROWS, ROWS)
        large.append(pltpu.make_async_copy(q_hbm.at[rows], q_ref.at[rows], sem.at[c]))
        large[-1].start()
    small[1].wait()
    vm = jnp.concatenate([v_ref[0], v_ref[1]], axis=0).astype(F32)
    mine = (iota((8, ELEMS), 1) >> 4) == iota((8, ELEMS), 0)
    spread = mark(iota((EZ, ELEMS), 0) == (iota((EZ, ELEMS), 1) & (EZ - 1)))
    vm_row = jnp.sum(jnp.where(mine, dot_onehot(vm, spread), 0.0), axis=0, keepdims=True)
    small[2].wait()
    scales = []
    for level in range(LEVELS):
        value = m_ref[0:1, level : level + 1].astype(F32) * factor(level)
        scales.append(jnp.broadcast_to(value, (1, 128)))
        aux_ref[level : level + 1, :] = scales[-1]
    aux_ref[LEVELS : LEVELS + 1, :] = vm_row
    small[0].wait()
    sums = []
    for a in range(EX):
        total = r_ref[a * NP]
        for i in range(1, NP):
            total = total + r_ref[a * NP + i]
        sums.append(jnp.sum(total.reshape(EY, NP, NZ), axis=1))
    sums = jnp.concatenate(sums, axis=0) * (1.0 / NP**3)
    gather = mark((iota((NZ, ELEMS), 0) >> 3) == (iota((NZ, ELEMS), 1) & (EZ - 1)))
    means = jnp.sum(jnp.where(mine, dot_onehot(sums, gather), 0.0), axis=0, keepdims=True)
    aux_ref[LEVELS + 1 : LEVELS + 2, :] = means
    for g, value in enumerate(vertex_values(vm_row, means)):
        b_ref[g * 8 : g * 8 + 8, :] = jnp.broadcast_to(value, (8, 128))
    flat = r_ref[...].reshape(NX * NY, NZ)
    row, lane = iota((8, NZ), 0), iota((8, NZ), 1)
    side = odd("gz")
    lane_a = (1 - side) * (NZ - 1)
    lane_b = side * (NZ - 1)
    pick = mark(((row == 0) & (lane == lane_a)) | ((row == 1) & (lane == lane_b)))
    faces = dot(pick, flat, NT)
    for k in range(4):
        face_a_ref[k : k + 1, :] = faces[0:1, k * 128 : (k + 1) * 128]
        face_b_ref[k : k + 1, :] = faces[1:2, k * 128 : (k + 1) * 128]
    acc = [jnp.zeros((8, 128), F32) for _ in range(PARTIALS)]
    for c in range(CHUNKS):
        large[c].wait()
        for g in range(ROWS // 8):
            at = c * ROWS + g * 8
            b = b_ref[at : at + 8, :]
            for t in range(PARTIALS):
                acc[t] = acc[t] + q_ref[at : at + 8, t * 128 : (t + 1) * 128] * b
    for t in range(PARTIALS):
        total = jnp.sum(acc[t], axis=0, keepdims=True) * scales[t // TILES]
        out_ref[t : t + 1, :] = total
        if t >= LAST:
            face_a_ref[4 + t - LAST : 5 + t - LAST, :] = total
    for copy in small[3:]:
        copy.wait()


def edge_kernel(r_ref, za_ref, zb_ref, partial_ref, a_ref, b_ref):
    side = odd("gz")
    za, zb = za_ref[0:4, :], zb_ref[...]
    low = jnp.where(side == 1, za, zb)
    high = jnp.where(side == 1, zb, za)
    turned = odd("xy") == 1
    first, last = r_ref[0], r_ref[NX - 1]
    for out, take in ((a_ref, turned), (b_ref, jnp.logical_not(turned))):
        out[0:NY, :] = jnp.where(take, first, last)
        out[NY:FACE, :] = jnp.zeros((8, NZ), F32)
        for i, edge in enumerate((low, high)):
            out[NY + i : NY + i + 1, 0:NY] = jnp.where(take, edge[0:1, 0:NY], edge[3:4, 128 - NY :])
    a_ref[FACE : FACE + PARTIALS, :] = partial_ref[...]


def middle_kernel(scale_ref, alpha_ref, leaf_ref, q_ref, out_ref):
    acc = [jnp.zeros((8, 128), F32) for _ in range(TILES)]
    values = vertex_values(scale_ref[LEVELS : LEVELS + 1, :], scale_ref[LEVELS + 1 : LEVELS + 2, :])
    for g, b in enumerate(values):
        for t in range(TILES):
            acc[t] = acc[t] + leaf_ref[g * 8 : g * 8 + 8, t * 128 : (t + 1) * 128] * b
    leaf_alpha = [jnp.sum(acc[t], axis=0, keepdims=True) for t in range(TILES)]
    alpha = []
    for t in range((LEVELS - 1) * TILES):
        level = t // TILES
        alpha.append(alpha_ref[t : t + 1, :] * scale_ref[level : level + 1, :])
    for c in range(CHUNKS):
        rows = slice(c * ROWS, (c + 1) * ROWS)
        total = leaf_ref[rows, 0:128] * leaf_alpha[0]
        for t in range(1, TILES):
            total = total + leaf_ref[rows, t * 128 : (t + 1) * 128] * leaf_alpha[t]
        for t in range(len(alpha)):
            total = total + q_ref[rows, t * 128 : (t + 1) * 128] * alpha[t]
        out_ref[rows, :] = total


def final_kernel(scale_ref, alpha_ref, base_ref, low_ref, high_ref, q_ref, out_ref, sol_ref):
    alpha = alpha_ref[...] * scale_ref[LEVELS - 1 : LEVELS, :]
    start = (LEVELS - 1) * SW
    vm_row = scale_ref[LEVELS : LEVELS + 1, :]
    acc = jnp.zeros((8, ELEMS), F32)
    totals = []
    for g in range(VERTS // 8):
        rows = slice(g * 8, g * 8 + 8)
        total = base_ref[rows, :]
        for t in range(TILES):
            at = start + t * 128
            total = total + q_ref[rows, at : at + 128] * alpha[t : t + 1, :]
        totals.append(total)
        value = jnp.sum(total, axis=1, keepdims=True)
        vertex = (iota((8, ELEMS), 0) + g * 8).astype(F32)
        acc = acc + jnp.where(vertex == vm_row, value, 0.0)
    per_element = jnp.sum(acc, axis=0, keepdims=True)
    mine = (iota((8, ELEMS), 1) >> 4) == iota((8, ELEMS), 0)
    spread = mark((iota((ELEMS, NZ), 0) & (EZ - 1)) == (iota((ELEMS, NZ), 1) >> 3))
    rows = dot_onehot(jnp.where(mine, per_element, 0.0), spread)
    for a, local_ref in enumerate((low_ref, high_ref)):
        add = jnp.broadcast_to(rows[a * EY : (a + 1) * EY, None, :], (EY, NP, NZ)).reshape(NY, NZ)
        for i in range(NP):
            out_ref[a * NP + i] = local_ref[i] + add
    ones = jnp.ones((8, 128), BF16)
    row = [bdot(ones, part.astype(BF16), NT) for part in split3(jnp.concatenate(totals, axis=0))]
    sol_ref[...] = (row[0] + (row[1] + row[2]))[0:1]


LZ = EZ * PTS
LXY = PTS * EY * PTS


def prep_kernel(
    lam_ref, vec_ref, scale_ref, bz0_ref, bz1_ref, in0_ref, in1_ref, f0_ref, f1_ref, k0_ref, k1_ref, inv_ref
):
    lane = iota((NZ + 8, LZ), 1)
    z = iota((NZ + 8, LZ), 0)
    c, p = div_mod(lane, PTS)
    z = jnp.where(z < NZ, z, jnp.where(z == NZ, -1, jnp.where(z == NZ + 1, NZ, -1000)))
    place = z - NP * c + 1
    _, p10 = div_mod(iota((PTS, LZ), 1), PTS)
    repeat = mark(p10 == iota((PTS, LZ), 0))
    v2 = dot(vec_ref[:, 2, :], repeat)
    bz = jnp.zeros((NZ + 8, LZ), F32)
    for k in range(PTS):
        bz = jnp.where(place == k, v2[k : k + 1, :], bz)
    bz_in = jnp.where((place >= 1) & (place <= NP), bz, 0.0)[0:NZ]
    bz0_ref[...], bz1_ref[...] = split(bz)
    in0_ref[...], in1_ref[...] = split(bz_in)

    _, n = div_mod(iota((PTS, LXY), 1), PTS)
    m, _ = div_mod(iota((PTS, LXY), 1), PTS * EY)
    at = iota((PTS, LXY), 0)
    v1 = dot(vec_ref[:, 1, :], mark(n == at))
    v0 = dot(vec_ref[:, 0, :], mark(m == at))
    mb, _ = div_mod(iota((NY, LXY), 1), PTS)
    b = mb & (EY - 1)
    y = iota((NY, LXY), 0)
    place = y - NP * b + 1
    by = jnp.zeros((NY, LXY), F32)
    for j in range(PTS):
        by = jnp.where(place == j, v1[j : j + 1, :], by)
    by_in = jnp.where((place >= 1) & (place <= NP), by, 0.0)
    forward = jnp.concatenate([by * v0[i : i + 1, :] for i in range(PTS)], axis=0)
    f0_ref[...], f1_ref[...] = split(forward.T)
    back = jnp.concatenate([by_in * v0[i : i + 1, :] for i in range(1, NP + 1)], axis=0)
    k0_ref[...], k1_ref[...] = split(back)

    rows40 = EY * PTS
    rb, _ = div_mod(iota((rows40, EY), 0), PTS)
    pick_b = mark(rb == iota((rows40, EY), 1))
    lc, _ = div_mod(iota((EZ, LZ), 1), PTS)
    pick_c = mark(lc == iota((EZ, LZ), 0))
    _, rn = div_mod(iota((rows40, LZ), 0), PTS)
    _, lp = div_mod(iota((rows40, LZ), 1), PTS)
    lam = jnp.zeros((rows40, LZ), F32)
    lam2 = jnp.zeros((rows40, LZ), F32)
    for k in range(PTS):
        lam = jnp.where(rn == k, lam_ref[1:2, k : k + 1], lam)
        lam2 = jnp.where(lp == k, lam_ref[2:3, k : k + 1], lam2)
    for a in range(EX):
        factors = dot(dot(pick_b, scale_ref[a]), pick_c)
        for i in range(PTS):
            inv_ref[a, i * rows40 : (i + 1) * rows40, :] = 1.0 / (
                factors * ((lam_ref[0:1, i : i + 1] + lam) + lam2)
            )


def local_kernel(
    a, r_ref, za_ref, zb_ref, xa_ref, xb_ref,
    bz0_ref, bz1_ref, in0_ref, in1_ref, f0_ref, f1_ref, k0_ref, k1_ref, inv_ref, out_ref,
):
    row = iota((8, 128), 0)
    side = odd("gz")
    za, zb = za_ref[0:4, :], zb_ref[...]
    zlow, zhigh = jnp.where(side == 1, za, zb), jnp.where(side == 1, zb, za)
    turned = odd("xy") == 1
    xa, xb = xa_ref[0:FACE, :], xb_ref[...]
    xlow, xhigh = jnp.where(turned, xa, xb), jnp.where(turned, xb, xa)
    sides = [
        jnp.where(row == 0, zlow[k : k + 1], jnp.where(row == 1, zhigh[k : k + 1], 0.0)).T
        for k in range(4)
    ]
    sides = jnp.concatenate([xlow[NY:FACE].T[0:NY], *sides, xhigh[NY:FACE].T[0:NY]], axis=0)
    points = jnp.concatenate([xlow[0:NY], r_ref[...].reshape(NX * NY, NZ), xhigh[0:NY]], axis=0)
    points = jnp.concatenate([points, sides], axis=1)[a * NP * NY : (a * NP + PTS) * NY]
    window = split(dot3(split(points), (bz0_ref[...], bz1_ref[...])))
    scaled = dot3((f0_ref[...], f1_ref[...]), window) * inv_ref[a]
    inner = dot3((k0_ref[...], k1_ref[...]), split(scaled))
    result = dot3(split(inner), (in0_ref[...], in1_ref[...]), NT)
    out_ref[...] = result.reshape(NP, NY, NZ)


def shape(*dims):
    return jax.ShapeDtypeStruct(dims, F32)


def cost(flops, size):
    return pl.CostEstimate(flops=flops, bytes_accessed=size, transcendentals=0)


def per_device(
    residual,
    eigen_vectors,
    eigen_values,
    element_scale,
    vertex_map,
    leaf_columns,
    separator_columns,
    separator_mask,
):
    face_a, face_b, partial, aux, points, separators, vectors, values, scale = pl.pallas_call(
        first_kernel,
        out_shape=(
            shape(8, 128), shape(4, 128), shape(PARTIALS, 128), shape(8, 128),
            shape(NX, NY, NZ), shape(VERTS, LEVELS * SW),
            shape(PTS, 3, PTS), shape(3, PTS), shape(EX, EY, EZ),
        ),
        in_specs=[pl.BlockSpec(memory_space=pltpu.HBM)] * 7,
        out_specs=(VMEM,) * 9,
        scratch_shapes=[
            pltpu.VMEM((EX, EY, EZ), jnp.int32),
            pltpu.VMEM((1, LEVELS), jnp.int32),
            pltpu.VMEM((VERTS, 128), F32),
            pltpu.SemaphoreType.DMA((CHUNKS + 6,)),
        ],
        compiler_params=pltpu.CompilerParams(vmem_limit_bytes=FIRST_LIMIT),
        cost_estimate=cost(6 * 512 * 512 * 2, 6_500_000),
        name="first",
    )(
        *(
            pltpu.with_memory_space_constraint(x, pltpu.HBM)
            for x in (
                residual, vertex_map, separator_mask, separator_columns,
                eigen_vectors.transpose(1, 0, 2), eigen_values, element_scale,
            )
        )
    )

    def swap(value, axis, bits):
        return lax.ppermute(value, axis, [(i, i ^ bits) for i in range(lax.axis_size(axis))])

    def pairs(value, axis):
        odds = range(1, lax.axis_size(axis) - 1, 2)
        return lax.ppermute(value, axis, [p for i in odds for p in ((i, i + 1), (i + 1, i))])

    z_a = swap(face_a, "gz", 1)
    z_b = pairs(face_b, "gz")

    last = partial[LAST:] + z_a[4:]
    total = jnp.concatenate([partial[:LAST], last], axis=0)

    message_a, message_b = pl.pallas_call(
        edge_kernel,
        out_shape=(shape(FACE + PARTIALS, NZ), shape(FACE, NZ)),
        in_specs=[VMEM] * 4,
        out_specs=(VMEM, VMEM),
        compiler_params=PARAMS,
        cost_estimate=cost(1000, 100_000),
        name="edges",
    )(points, z_a, z_b, total)

    level = jnp.arange(PARTIALS, dtype=jnp.int32)[:, None] // TILES

    def from_level(value, first):
        return jnp.where(level >= first, value, 0.0)

    two, three = swap(total, "xy", 2), swap(total, "xy", 3)
    x_a = swap(message_a, "xy", 1)
    x_b = pairs(message_b, "xy")
    total = total + x_a[FACE:] + from_level(two + three, 1)
    total, x_b = lax.optimization_barrier((total, x_b))
    total = total + from_level(swap(total, "xy", 6), 2)
    half = lambda *dims: jax.ShapeDtypeStruct(dims, BF16)
    matrices = pl.pallas_call(
        prep_kernel,
        out_shape=(half(NZ + 8, LZ),) * 2
        + (half(NZ, LZ),) * 2
        + (half(LXY, PTS * NY),) * 2
        + (half(NP * NY, LXY),) * 2
        + (shape(EX, LXY, LZ),),
        in_specs=[VMEM] * 3,
        out_specs=(VMEM,) * 9,
        compiler_params=PARAMS,
        cost_estimate=cost(1_000_000_000, 1_000_000),
        name="prep",
    )(values, vectors, scale)
    total, matrices = lax.optimization_barrier((total, matrices))
    one, two, three = (swap(total, "xy", bits) for bits in (8, 16, 24))
    total = total + from_level(one, 3) + from_level(two + three, 4)

    def local(a):
        return pl.pallas_call(
            functools.partial(local_kernel, a),
            out_shape=shape(NP, NY, NZ),
            in_specs=[VMEM] * 14,
            out_specs=VMEM,
            compiler_params=PARAMS,
            cost_estimate=cost(1_000_000_000, 1_000_000),
            name="local",
        )(points, z_a, z_b, x_a, x_b, *matrices)

    low = local(0)
    total, low = lax.optimization_barrier((total, low))
    last = total[LAST:]
    last = last + (swap(last, "gz", 2) + swap(last, "gz", 4) + swap(last, "gz", 6))
    high = local(1)
    base = pl.pallas_call(
        middle_kernel,
        out_shape=shape(VERTS, 128),
        in_specs=[VMEM] * 4,
        out_specs=VMEM,
        compiler_params=PARAMS,
        cost_estimate=cost(7 * 512 * 512 * 2, 7_000_000),
        name="middle",
    )(aux, total, leaf_columns, separators)

    out, sol = pl.pallas_call(
        final_kernel,
        out_shape=(shape(NX, NY, NZ), shape(1, VERTS)),
        in_specs=[VMEM] * 6,
        out_specs=(VMEM, VMEM),
        compiler_params=PARAMS,
        cost_estimate=cost(512 * 512 * 2, 1_500_000),
        name="final",
    )(aux, last, base, low, high, separators)
    return out, sol.reshape(VERTS)


def solution(mesh):
    placed = (
        P("xy", None, "gz"),
        P(),
        P(),
        P("xy", None, "gz"),
        P("xy", None, "gz"),
        P(("gz", "xy"), None),
        P(("gz", "xy"), None),
        P(("gz", "xy"), None),
    )
    return jax.shard_map(
        per_device,
        mesh=mesh,
        in_specs=placed,
        out_specs=(P("xy", None, "gz"), P(("gz", "xy"))),
        check_vma=False,
    )
```

profile of v0, /device:TPU:2, one launch (start us, length us, event | category | flops | bytes accessed | tf_op | source)
XLA Modules:
  0.0 43.9 jit_solution(8409099369069290737)
XLA Ops:
  0.6 3.2 %first.1 = (f32[8,128]{1,0:T(8,128)S(1)}, f32[4,128]{1,0:T(4,128)S(1)}, f32[24,128]{1,0:T(8,128)S(1)}, f32[8,128]{1,0:T(8,128)S(1)}, f32[16,32,128]{2,1,0:T(8,12...) custom-call(f32[16,32,128]{2,1,0:T(8,128)} %r_hbm.1, ...), custom_call_target="tpu_custom_call" | custom-call | flops 3145728 | bytes 6500000 | tf_op jit(solution)/shard_map/first/pallas_call | solution.py:338
  3.8 0.0 copy-start
  3.8 2.1 %collective-permute-start.1 = (f32[4,128]{1,0:T(4,128)S(1)}, f32[4,128]{1,0:T(4,128)S(1)}, u32[]{:S(2)}, u32[]{:S(2)}) collective-permute-start(f32[4,128]{1,0:T(4,128)S(1)} %get-tuple-element.42), channel_id=1, source_target_pairs={{32,64},{64,32},{96,128},{128,96},{160,192},{192,160},{33,65},{65,... | collective-permute-start | bytes 6152 | tf_op jit(solution)/shard_map/ppermute | solution.py:371
  5.9 1.7 %collective-permute-start = (f32[8,128]{1,0:T(8,128)S(1)}, f32[8,128]{1,0:T(8,128)S(1)}, u32[]{:S(2)}, u32[]{:S(2)}) collective-permute-start(f32[8,128]{1,0:T(8,128)S(1)} %get-tuple-element.40), channel_id=1, source_target_pairs={{0,32},{32,0},{64,96},{96,64},{128,160},{160,128},{192,224},{224,1... | collective-permute-start | bytes 12296 | tf_op jit(solution)/shard_map/ppermute | solution.py:367
  7.6 0.8 %collective-permute-done.za_ref = f32[8,128]{1,0:T(8,128)S(1)} collective-permute-done((f32[8,128]{1,0:T(8,128)S(1)}, f32[8,128]{1,0:T(8,128)S(1)}, u32[]{:S(2)}, u32[]{:S(2)}) %collective-permute-start) | collective-permute-done | bytes 4128 | tf_op jit(solution)/shard_map/ppermute | solution.py:367
  8.4 3.4 %collective-permute-start.3 = (f32[24,128]{1,0:T(8,128)S(1)}, f32[24,128]{1,0:T(8,128)S(1)}, u32[]{:S(2)}, u32[]{:S(2)}) collective-permute-start(f32[24,128]{1,0:T(8,128)S(1)} %pad_maximum_fusion.partial_ref), channel_id=1, source_target_pairs={{0,2},{1,3},{2,0},{3,1},{4,6},{5,7},{6,4},{7,5},{8,10},{9,11},{10,... | collective-permute-start | bytes 36872 | tf_op jit(solution)/shard_map/ppermute | solution.py:367
  11.8 1.5 %collective-permute-start.4 = (f32[24,128]{1,0:T(8,128)S(1)}, f32[24,128]{1,0:T(8,128)S(1)}, u32[]{:S(2)}, u32[]{:S(2)}) collective-permute-start(f32[24,128]{1,0:T(8,128)S(1)} %pad_maximum_fusion.partial_ref), channel_id=1, source_target_pairs={{0,3},{1,2},{2,1},{3,0},{4,7},{5,6},{6,5},{7,4},{8,11},{9,10},{10,... | collective-permute-start | bytes 36872 | tf_op jit(solution)/shard_map/ppermute | solution.py:367
  13.2 0.0 collective-permute-done.1.zb_ref
  13.2 0.1 edges.1
  13.4 0.5 %collective-permute-start.2 = (f32[64,128]{1,0:T(8,128)S(1)}, f32[64,128]{1,0:T(8,128)S(1)}, u32[]{:S(2)}, u32[]{:S(2)}) collective-permute-start(f32[64,128]{1,0:T(8,128)S(1)} %get-tuple-element.43), channel_id=1, source_target_pairs={{0,1},{1,0},{2,3},{3,2},{4,5},{5,4},{6,7},{7,6},{8,9},{9,8},{10,11... | collective-permute-start | bytes 98312 | tf_op jit(solution)/shard_map/ppermute | solution.py:367
  13.8 0.7 %collective-permute-start.5 = (f32[40,128]{1,0:T(8,128)S(1)}, f32[40,128]{1,0:T(8,128)S(1)}, u32[]{:S(2)}, u32[]{:S(2)}) collective-permute-start(f32[40,128]{1,0:T(8,128)S(1)} %get-tuple-element.44), channel_id=1, source_target_pairs={{1,2},{2,1},{3,4},{4,3},{5,6},{6,5},{7,8},{8,7},{9,10},{10,9},{11,... | collective-permute-start | bytes 61448 | tf_op jit(solution)/shard_map/ppermute | solution.py:371
  14.5 0.0 collective-permute-done.3
  14.5 2.9 %collective-permute-done.4 = f32[24,128]{1,0:T(8,128)S(1)} collective-permute-done((f32[24,128]{1,0:T(8,128)S(1)}, f32[24,128]{1,0:T(8,128)S(1)}, u32[]{:S(2)}, u32[]{:S(2)}) %collective-permute-start.4) | collective-permute-done | bytes 12320 | tf_op jit(solution)/shard_map/ppermute | solution.py:367
  17.4 0.0 collective-permute-done.2.xa_ref
  17.4 0.1 fusion
  17.5 0.0 collective-permute-done.5.xb_ref
  17.5 7.5 %collective-permute-start.6 = (f32[24,128]{1,0:T(8,128)S(1)}, f32[24,128]{1,0:T(8,128)S(1)}, u32[]{:S(2)}, u32[]{:S(2)}) collective-permute-start(f32[24,128]{1,0:T(8,128)S(1)} %fusion), channel_id=1, source_target_pairs={{0,6},{1,7},{2,4},{3,5},{4,2},{5,3},{6,0},{7,1},{8,14},{9,15},{10,... | collective-permute-start | bytes 36872 | tf_op jit(solution)/shard_map/ppermute | solution.py:367
  25.0 1.1 %prep.1 = (bf16[136,160]{1,0:T(8,128)(2,1)S(1)}, bf16[136,160]{1,0:T(8,128)(2,1)S(1)}, bf16[128,160]{1,0:T(8,128)(2,1)S(1)}, bf16[128,160]{1,0:T(8,128)(2,1)S(1)...) custom-call(f32[3,10]{1,0:T(4,128)S(1)} %get-tuple-element.46.lam_re, ...), custom_call_target="tpu_custom_call" | custom-call | flops 1000000000 | bytes 1000000 | tf_op jit(solution)/shard_map/prep/pallas_call | solution.py:401
  26.1 0.5 %collective-permute-done.6 = f32[24,128]{1,0:T(8,128)S(1)} collective-permute-done((f32[24,128]{1,0:T(8,128)S(1)}, f32[24,128]{1,0:T(8,128)S(1)}, u32[]{:S(2)}, u32[]{:S(2)}) %collective-permute-start.6) | collective-permute-done | bytes 12320 | tf_op jit(solution)/shard_map/ppermute | solution.py:367
  26.7 0.1 select_add_fusion.1
  26.7 4.0 %collective-permute-start.9 = (f32[24,128]{1,0:T(8,128)S(1)}, f32[24,128]{1,0:T(8,128)S(1)}, u32[]{:S(2)}, u32[]{:S(2)}) collective-permute-start(f32[24,128]{1,0:T(8,128)S(1)} %select_add_fusion.1), channel_id=1, source_target_pairs={{0,24},{1,25},{2,26},{3,27},{4,28},{5,29},{6,30},{7,31},{8,16},{9,... | collective-permute-start | bytes 36872 | tf_op jit(solution)/shard_map/ppermute | solution.py:367
  30.7 0.4 collective-permute-start.8
  31.2 0.5 %collective-permute-start.7 = (f32[24,128]{1,0:T(8,128)S(1)}, f32[24,128]{1,0:T(8,128)S(1)}, u32[]{:S(2)}, u32[]{:S(2)}) collective-permute-start(f32[24,128]{1,0:T(8,128)S(1)} %select_add_fusion.1), channel_id=1, source_target_pairs={{0,8},{1,9},{2,10},{3,11},{4,12},{5,13},{6,14},{7,15},{8,0},{9,1},... | collective-permute-start | bytes 36872 | tf_op jit(solution)/shard_map/ppermute | solution.py:367
  31.7 1.8 %local.2.low_ref = f32[8,32,128]{2,1,0:T(8,128)S(1)} custom-call(f32[16,32,128]{2,1,0:T(8,128)S(1)} %get-tuple-element.41.r_ref, f32[8,128]{1,0:T(8,128)S(1)} %collective-permute-done.za_ref, f32[4,128]{1,0:T(4,128)S(1)} %collective-permute-done.1.zb_ref, f32[64,128]{1,0:T(8,128)S(1)} %collective-permute-done.2.xa_ref, ...), custom_call_target="tpu_custom_call" | custom-call | flops 1000000000 | bytes 1000000 | tf_op jit(solution)/shard_map/local/pallas_call | solution.py:419
  33.5 0.0 collective-permute-done.9
  33.5 2.4 %collective-permute-done.8 = f32[24,128]{1,0:T(8,128)S(1)} collective-permute-done((f32[24,128]{1,0:T(8,128)S(1)}, f32[24,128]{1,0:T(8,128)S(1)}, u32[]{:S(2)}, u32[]{:S(2)}) %collective-permute-start.8) | collective-permute-done | bytes 12320 | tf_op jit(solution)/shard_map/ppermute | solution.py:367
  35.9 0.0 collective-permute-done.7
  35.9 0.1 select_add_fusion.alpha_ref
  36.0 1.3 %collective-permute-start.12 = (f32[4,128]{1,0:T(4,128)S(1)}, f32[4,128]{1,0:T(4,128)S(1)}, u32[]{:S(2)}, u32[]{:S(2)}) collective-permute-start(f32[4,128]{1,0:T(4,128)S(1)} %slice.19), channel_id=1, source_target_pairs={{0,192},{32,224},{64,128},{96,160},{128,64},{160,96},{192,0},{224,... | collective-permute-start | bytes 6152 | tf_op jit(solution)/shard_map/ppermute | solution.py:367
  37.3 1.4 %collective-permute-start.11 = (f32[4,128]{1,0:T(4,128)S(1)}, f32[4,128]{1,0:T(4,128)S(1)}, u32[]{:S(2)}, u32[]{:S(2)}) collective-permute-start(f32[4,128]{1,0:T(4,128)S(1)} %slice.19), channel_id=1, source_target_pairs={{0,128},{32,160},{64,192},{96,224},{128,0},{160,32},{192,64},{224,... | collective-permute-start | bytes 6152 | tf_op jit(solution)/shard_map/ppermute | solution.py:367
  38.7 1.5 %collective-permute-start.10 = (f32[4,128]{1,0:T(4,128)S(1)}, f32[4,128]{1,0:T(4,128)S(1)}, u32[]{:S(2)}, u32[]{:S(2)}) collective-permute-start(f32[4,128]{1,0:T(4,128)S(1)} %slice.19), channel_id=1, source_target_pairs={{0,64},{32,96},{64,0},{96,32},{128,192},{160,224},{192,128},{224,1... | collective-permute-start | bytes 6152 | tf_op jit(solution)/shard_map/ppermute | solution.py:367
  40.2 1.9 %local.3.high_ref = f32[8,32,128]{2,1,0:T(8,128)S(1)} custom-call(f32[16,32,128]{2,1,0:T(8,128)S(1)} %get-tuple-element.41.r_ref, f32[8,128]{1,0:T(8,128)S(1)} %collective-permute-done.za_ref, f32[4,128]{1,0:T(4,128)S(1)} %collective-permute-done.1.zb_ref, f32[64,128]{1,0:T(8,128)S(1)} %collective-permute-done.2.xa_ref, ...), custom_call_target="tpu_custom_call" | custom-call | flops 1000000000 | bytes 1000000 | tf_op jit(solution)/shard_map/local/pallas_call | solution.py:419
  42.1 0.0 copy-done
  42.1 0.8 %middle.1.base_ref = f32[512,128]{1,0:T(8,128)S(1)} custom-call(f32[8,128]{1,0:T(8,128)S(1)} %get-tuple-element.38.scale_ref, f32[24,128]{1,0:T(8,128)S(1)} %select_add_fusion.alpha_ref, f32[512,512]{1,0:T(8,128)S(1)} %copy-done, f32[512,3072]{1,0:T(8,128)S(1)} %get-tuple-element.70.q_ref), custom_call_target="tpu_custom_call" | custom-call | flops 3670016 | bytes 7000000 | tf_op jit(solution)/shard_map/middle/pallas_call | solution.py:434
  42.9 0.0 collective-permute-done.12
  42.9 0.0 collective-permute-done.11
  42.9 0.0 collective-permute-done.10
  42.9 1.0 %final.1 = (f32[16,32,128]{2,1,0:T(8,128)}, f32[1,512]{1,0:T(1,128)}) custom-call(f32[8,128]{1,0:T(8,128)S(1)} %get-tuple-element.38.scale_ref, f32[4,128]{1,0:T(4,128)S(1)} %add_add_fusion.alpha_ref, f32[512,128]{1,0:T(8,128)S(1)} %middle.1.base_ref, f32[8,32,128]{2,1,0:T(8,128)S(1)} %local.2.low_ref, f32[8,32,128]{2,1,0:T(8,128)S(1)} %local.3.high_ref, ...), custom_call_target="tpu_custom_call" | custom-call | flops 524288 | bytes 1500000 | tf_op jit(solution)/shard_map/final/pallas_call | solution.py:444
  (7 shorter events, 0.0 us)
Async XLA Ops:
  3.8 38.3 %copy-start = (f32[512,512]{1,0:T(8,128)S(1)}, f32[512,512]{1,0:T(8,128)}, u32[]{:S(2)}) copy-start(f32[512,512]{1,0:T(8,128)} %leaf_ref.1) | copy-start | bytes 3145732
  3.8 9.4 %collective-permute-start.1 = (f32[4,128]{1,0:T(4,128)S(1)}, f32[4,128]{1,0:T(4,128)S(1)}, u32[]{:S(2)}, u32[]{:S(2)}) collective-permute-start(f32[4,128]{1,0:T(4,128)S(1)} %get-tuple-element.42), channel_id=1, source_target_pairs={{32,64},{64,32},{96,128},{128,96},{160,192},{192,160},{33,65},{65,... | collective-permute-start | bytes 6152 | tf_op jit(solution)/shard_map/ppermute | solution.py:371
  5.9 2.5 %collective-permute-start = (f32[8,128]{1,0:T(8,128)S(1)}, f32[8,128]{1,0:T(8,128)S(1)}, u32[]{:S(2)}, u32[]{:S(2)}) collective-permute-start(f32[8,128]{1,0:T(8,128)S(1)} %get-tuple-element.40), channel_id=1, source_target_pairs={{0,32},{32,0},{64,96},{96,64},{128,160},{160,128},{192,224},{224,1... | collective-permute-start | bytes 12296 | tf_op jit(solution)/shard_map/ppermute | solution.py:367
  8.4 6.1 %collective-permute-start.3 = (f32[24,128]{1,0:T(8,128)S(1)}, f32[24,128]{1,0:T(8,128)S(1)}, u32[]{:S(2)}, u32[]{:S(2)}) collective-permute-start(f32[24,128]{1,0:T(8,128)S(1)} %pad_maximum_fusion.partial_ref), channel_id=1, source_target_pairs={{0,2},{1,3},{2,0},{3,1},{4,6},{5,7},{6,4},{7,5},{8,10},{9,11},{10,... | collective-permute-start | bytes 36872 | tf_op jit(solution)/shard_map/ppermute | solution.py:367
  11.8 5.6 %collective-permute-start.4 = (f32[24,128]{1,0:T(8,128)S(1)}, f32[24,128]{1,0:T(8,128)S(1)}, u32[]{:S(2)}, u32[]{:S(2)}) collective-permute-start(f32[24,128]{1,0:T(8,128)S(1)} %pad_maximum_fusion.partial_ref), channel_id=1, source_target_pairs={{0,3},{1,2},{2,1},{3,0},{4,7},{5,6},{6,5},{7,4},{8,11},{9,10},{10,... | collective-permute-start | bytes 36872 | tf_op jit(solution)/shard_map/ppermute | solution.py:367
  13.4 4.0 %collective-permute-start.2 = (f32[64,128]{1,0:T(8,128)S(1)}, f32[64,128]{1,0:T(8,128)S(1)}, u32[]{:S(2)}, u32[]{:S(2)}) collective-permute-start(f32[64,128]{1,0:T(8,128)S(1)} %get-tuple-element.43), channel_id=1, source_target_pairs={{0,1},{1,0},{2,3},{3,2},{4,5},{5,4},{6,7},{7,6},{8,9},{9,8},{10,11... | collective-permute-start | bytes 98312 | tf_op jit(solution)/shard_map/ppermute | solution.py:367
  13.8 3.6 %collective-permute-start.5 = (f32[40,128]{1,0:T(8,128)S(1)}, f32[40,128]{1,0:T(8,128)S(1)}, u32[]{:S(2)}, u32[]{:S(2)}) collective-permute-start(f32[40,128]{1,0:T(8,128)S(1)} %get-tuple-element.44), channel_id=1, source_target_pairs={{1,2},{2,1},{3,4},{4,3},{5,6},{6,5},{7,8},{8,7},{9,10},{10,9},{11,... | collective-permute-start | bytes 61448 | tf_op jit(solution)/shard_map/ppermute | solution.py:371
  17.5 9.2 %collective-permute-start.6 = (f32[24,128]{1,0:T(8,128)S(1)}, f32[24,128]{1,0:T(8,128)S(1)}, u32[]{:S(2)}, u32[]{:S(2)}) collective-permute-start(f32[24,128]{1,0:T(8,128)S(1)} %fusion), channel_id=1, source_target_pairs={{0,6},{1,7},{2,4},{3,5},{4,2},{5,3},{6,0},{7,1},{8,14},{9,15},{10,... | collective-permute-start | bytes 36872 | tf_op jit(solution)/shard_map/ppermute | solution.py:367
  26.7 6.8 %collective-permute-start.9 = (f32[24,128]{1,0:T(8,128)S(1)}, f32[24,128]{1,0:T(8,128)S(1)}, u32[]{:S(2)}, u32[]{:S(2)}) collective-permute-start(f32[24,128]{1,0:T(8,128)S(1)} %select_add_fusion.1), channel_id=1, source_target_pairs={{0,24},{1,25},{2,26},{3,27},{4,28},{5,29},{6,30},{7,31},{8,16},{9,... | collective-permute-start | bytes 36872 | tf_op jit(solution)/shard_map/ppermute | solution.py:367
  30.7 5.2 %collective-permute-start.8 = (f32[24,128]{1,0:T(8,128)S(1)}, f32[24,128]{1,0:T(8,128)S(1)}, u32[]{:S(2)}, u32[]{:S(2)}) collective-permute-start(f32[24,128]{1,0:T(8,128)S(1)} %select_add_fusion.1), channel_id=1, source_target_pairs={{0,16},{1,17},{2,18},{3,19},{4,20},{5,21},{6,22},{7,23},{8,24},{9,... | collective-permute-start | bytes 36872 | tf_op jit(solution)/shard_map/ppermute | solution.py:367
  31.2 4.8 %collective-permute-start.7 = (f32[24,128]{1,0:T(8,128)S(1)}, f32[24,128]{1,0:T(8,128)S(1)}, u32[]{:S(2)}, u32[]{:S(2)}) collective-permute-start(f32[24,128]{1,0:T(8,128)S(1)} %select_add_fusion.1), channel_id=1, source_target_pairs={{0,8},{1,9},{2,10},{3,11},{4,12},{5,13},{6,14},{7,15},{8,0},{9,1},... | collective-permute-start | bytes 36872 | tf_op jit(solution)/shard_map/ppermute | solution.py:367
  36.0 6.8 %collective-permute-start.12 = (f32[4,128]{1,0:T(4,128)S(1)}, f32[4,128]{1,0:T(4,128)S(1)}, u32[]{:S(2)}, u32[]{:S(2)}) collective-permute-start(f32[4,128]{1,0:T(4,128)S(1)} %slice.19), channel_id=1, source_target_pairs={{0,192},{32,224},{64,128},{96,160},{128,64},{160,96},{192,0},{224,... | collective-permute-start | bytes 6152 | tf_op jit(solution)/shard_map/ppermute | solution.py:367
  37.3 5.6 %collective-permute-start.11 = (f32[4,128]{1,0:T(4,128)S(1)}, f32[4,128]{1,0:T(4,128)S(1)}, u32[]{:S(2)}, u32[]{:S(2)}) collective-permute-start(f32[4,128]{1,0:T(4,128)S(1)} %slice.19), channel_id=1, source_target_pairs={{0,128},{32,160},{64,192},{96,224},{128,0},{160,32},{192,64},{224,... | collective-permute-start | bytes 6152 | tf_op jit(solution)/shard_map/ppermute | solution.py:367
  38.7 4.2 %collective-permute-start.10 = (f32[4,128]{1,0:T(4,128)S(1)}, f32[4,128]{1,0:T(4,128)S(1)}, u32[]{:S(2)}, u32[]{:S(2)}) collective-permute-start(f32[4,128]{1,0:T(4,128)S(1)} %slice.19), channel_id=1, source_target_pairs={{0,64},{32,96},{64,0},{96,32},{128,192},{160,224},{192,128},{224,1... | collective-permute-start | bytes 6152 | tf_op jit(solution)/shard_map/ppermute | solution.py:367
where the time goes:
time: 44.1 us; the launch traced here: 43.9 us
  starting transfers between devices  26.3 us (60%)
  Pallas kernels  9.91 us (22%)
  waiting for transfers between devices  6.66 us (15%)
  between operations  0.77 us (2%)
    ppermute x11, starting transfers between devices, swap(): lax.ppermute(value, axis, [(i, i ^ bits) for i in range(lax.axis_size(axi...  23.6 us
    ppermute x11, waiting for transfers between devices, swap(): lax.ppermute(value, axis, [(i, i ^ bits) for i in range(lax.axis_size(axi...  6.66 us
    pallas_call x2, Pallas kernels, local(): pl.pallas_call(functools.partial(local_kernel, a), out_shape=shape(NP, NY...  3.7 us
    pallas_call x1, Pallas kernels, per_device(): pl.pallas_call(first_kernel, out_shape=(shape(8, 128), shape(4, 128), sha...  3.17 us
    ppermute x2, starting transfers between devices, pairs(): lax.ppermute(value, axis, [p for i in odds for p in ((i, i + 1), (i + 1,...  2.7 us
    pallas_call x1, Pallas kernels, per_device(): pl.pallas_call(prep_kernel, out_shape=(half(NZ + 8, LZ),) * 2 + (half(NZ,...  1.12 us
    pallas_call x1, Pallas kernels, per_device(): pl.pallas_call(final_kernel, out_shape=(shape(NX, NY, NZ), shape(1, VERTS...  1.02 us
  transfers between devices with their start and end apart: 13, of which 4 were waited for; matrix products, arithmetic and copies ran while one was open for 0% of the time, Pallas kernels for 13%

commit v1 on v0

--- a/solution.py
+++ b/solution.py
@@ -75,6 +75,11 @@
 
 def odd(axis):
     return lax.rem(lax.axis_index(axis), 2)
+
+
+def inside(axis, value):
+    at = lax.axis_index(axis)
+    return jnp.where((at > 0) & (at < lax.axis_size(axis) - 1), value, 0.0)
 
 
 def factor(level):
@@ -169,7 +174,7 @@
 
 def edge_kernel(r_ref, za_ref, zb_ref, partial_ref, a_ref, b_ref):
     side = odd("gz")
-    za, zb = za_ref[0:4, :], zb_ref[...]
+    za, zb = za_ref[0:4, :], inside("gz", zb_ref[...])
     low = jnp.where(side == 1, za, zb)
     high = jnp.where(side == 1, zb, za)
     turned = odd("xy") == 1
@@ -203,7 +208,7 @@
         out_ref[rows, :] = total
 
 
-def final_kernel(scale_ref, alpha_ref, base_ref, low_ref, high_ref, q_ref, out_ref, sol_ref):
+def final_kernel(scale_ref, alpha_ref, base_ref, near_ref, far_ref, q_ref, out_ref, sol_ref):
     alpha = alpha_ref[...] * scale_ref[LEVELS - 1 : LEVELS, :]
     start = (LEVELS - 1) * SW
     vm_row = scale_ref[LEVELS : LEVELS + 1, :]
@@ -223,10 +228,12 @@
     mine = (iota((8, ELEMS), 1) >> 4) == iota((8, ELEMS), 0)
     spread = mark((iota((ELEMS, NZ), 0) & (EZ - 1)) == (iota((ELEMS, NZ), 1) >> 3))
     rows = dot_onehot(jnp.where(mine, per_element, 0.0), spread)
-    for a, local_ref in enumerate((low_ref, high_ref)):
+    turned = odd("xy") == 1
+    for a in range(EX):
         add = jnp.broadcast_to(rows[a * EY : (a + 1) * EY, None, :], (EY, NP, NZ)).reshape(NY, NZ)
         for i in range(NP):
-            out_ref[a * NP + i] = local_ref[i] + add
+            local = jnp.where(turned == (a == 0), near_ref[i], far_ref[i])
+            out_ref[a * NP + i] = local + add
     ones = jnp.ones((8, 128), BF16)
     row = [bdot(ones, part.astype(BF16), NT) for part in split3(jnp.concatenate(totals, axis=0))]
     sol_ref[...] = (row[0] + (row[1] + row[2]))[0:1]
@@ -293,25 +300,37 @@
 
 
 def local_kernel(
-    a, r_ref, za_ref, zb_ref, xa_ref, xb_ref,
+    other, r_ref, za_ref, zb_ref, face_ref,
     bz0_ref, bz1_ref, in0_ref, in1_ref, f0_ref, f1_ref, k0_ref, k1_ref, inv_ref, out_ref,
 ):
     row = iota((8, 128), 0)
     side = odd("gz")
-    za, zb = za_ref[0:4, :], zb_ref[...]
+    za, zb = za_ref[0:4, :], inside("gz", zb_ref[...])
     zlow, zhigh = jnp.where(side == 1, za, zb), jnp.where(side == 1, zb, za)
-    turned = odd("xy") == 1
-    xa, xb = xa_ref[0:FACE, :], xb_ref[...]
-    xlow, xhigh = jnp.where(turned, xa, xb), jnp.where(turned, xb, xa)
+    face = face_ref[0:FACE, :]
+    if other:
+        face = inside("xy", face)
+    at = odd("xy") if other else 1 - odd("xy")
+    before = at == 0
     sides = [
         jnp.where(row == 0, zlow[k : k + 1], jnp.where(row == 1, zhigh[k : k + 1], 0.0)).T
         for k in range(4)
     ]
-    sides = jnp.concatenate([xlow[NY:FACE].T[0:NY], *sides, xhigh[NY:FACE].T[0:NY]], axis=0)
-    points = jnp.concatenate([xlow[0:NY], r_ref[...].reshape(NX * NY, NZ), xhigh[0:NY]], axis=0)
-    points = jnp.concatenate([points, sides], axis=1)[a * NP * NY : (a * NP + PTS) * NY]
+    edge = face[NY:FACE].T[0:NY]
+    own = r_ref[pl.ds(at * (NP - 1), NP + 1)].reshape((NP + 1) * NY, NZ)
+    sides = jnp.concatenate(sides, axis=0)
+    sides = jnp.where(before, sides[: (NP + 1) * NY], sides[(NP - 1) * NY :])
+    points = jnp.where(
+        before,
+        jnp.concatenate([face[0:NY], own], axis=0),
+        jnp.concatenate([own, face[0:NY]], axis=0),
+    )
+    sides = jnp.where(
+        before, jnp.concatenate([edge, sides], axis=0), jnp.concatenate([sides, edge], axis=0)
+    )
+    points = jnp.concatenate([points, sides], axis=1)
     window = split(dot3(split(points), (bz0_ref[...], bz1_ref[...])))
-    scaled = dot3((f0_ref[...], f1_ref[...]), window) * inv_ref[a]
+    scaled = dot3((f0_ref[...], f1_ref[...]), window) * inv_ref[at]
     inner = dot3((k0_ref[...], k1_ref[...]), split(scaled))
     result = dot3(split(inner), (in0_ref[...], in1_ref[...]), NT)
     out_ref[...] = result.reshape(NP, NY, NZ)
@@ -367,8 +386,8 @@
         return lax.ppermute(value, axis, [(i, i ^ bits) for i in range(lax.axis_size(axis))])
 
     def pairs(value, axis):
-        odds = range(1, lax.axis_size(axis) - 1, 2)
-        return lax.ppermute(value, axis, [p for i in odds for p in ((i, i + 1), (i + 1, i))])
+        count = lax.axis_size(axis)
+        return lax.ppermute(value, axis, [(i, (i + 2 * (i % 2) - 1) % count) for i in range(count)])
 
     z_a = swap(face_a, "gz", 1)
     z_b = pairs(face_b, "gz")
@@ -395,8 +414,6 @@
     x_a = swap(message_a, "xy", 1)
     x_b = pairs(message_b, "xy")
     total = total + x_a[FACE:] + from_level(two + three, 1)
-    total, x_b = lax.optimization_barrier((total, x_b))
-    total = total + from_level(swap(total, "xy", 6), 2)
     half = lambda *dims: jax.ShapeDtypeStruct(dims, BF16)
     matrices = pl.pallas_call(
         prep_kernel,
@@ -411,26 +428,29 @@
         cost_estimate=cost(1_000_000_000, 1_000_000),
         name="prep",
     )(values, vectors, scale)
-    total, matrices = lax.optimization_barrier((total, matrices))
-    one, two, three = (swap(total, "xy", bits) for bits in (8, 16, 24))
-    total = total + from_level(one, 3) + from_level(two + three, 4)
-
-    def local(a):
+
+    def local(other, face):
         return pl.pallas_call(
-            functools.partial(local_kernel, a),
+            functools.partial(local_kernel, other),
             out_shape=shape(NP, NY, NZ),
-            in_specs=[VMEM] * 14,
+            in_specs=[VMEM] * 13,
             out_specs=VMEM,
             compiler_params=PARAMS,
             cost_estimate=cost(1_000_000_000, 1_000_000),
             name="local",
-        )(points, z_a, z_b, x_a, x_b, *matrices)
-
-    low = local(0)
-    total, low = lax.optimization_barrier((total, low))
+        )(points, z_a, z_b, face, *matrices)
+
+    total, matrices = lax.optimization_barrier((total, matrices))
+    near = local(False, x_a)
+    total = total + from_level(swap(total, "xy", 6), 2)
+    total, near = lax.optimization_barrier((total, near))
+    far = local(True, x_b)
+    one, two, three = (swap(total, "xy", bits) for bits in (8, 16, 24))
+    total = total + from_level(one, 3) + from_level(two + three, 4)
+    total, far = lax.optimization_barrier((total, far))
     last = total[LAST:]
-    last = last + (swap(last, "gz", 2) + swap(last, "gz", 4) + swap(last, "gz", 6))
-    high = local(1)
+    last = last + (swap(last, "gz", 3) + swap(last, "gz", 5) + swap(last, "gz", 7))
+
     base = pl.pallas_call(
         middle_kernel,
         out_shape=shape(VERTS, 128),
@@ -449,7 +469,7 @@
         compiler_params=PARAMS,
         cost_estimate=cost(512 * 512 * 2, 1_500_000),
         name="final",
-    )(aux, last, base, low, high, separators)
+    )(aux, last, base, near, far, separators)
     return out, sol.reshape(VERTS)
 
 

time: 44.1 us -> 39.8 us (0.902)
  the two profiles are of different devices: /device:TPU:2 before, /device:TPU:1 now
where the time goes in v1:
time: 39.8 us; the launch traced here: 39.7 us
  starting transfers between devices  24.6 us (62%)
  Pallas kernels  9.99 us (25%)
  waiting for transfers between devices  4.06 us (10%)
  between operations  0.75 us (2%)
    ppermute x11, starting transfers between devices, swap(): lax.ppermute(value, axis, [(i, i ^ bits) for i in range(lax.axis_size(axi...  18.3 us
    ppermute x2, starting transfers between devices, pairs(): lax.ppermute(value, axis, [(i, (i + 2 * (i % 2) - 1) % count) for i in ra...  6.3 us
    ppermute x11, waiting for transfers between devices, swap(): lax.ppermute(value, axis, [(i, i ^ bits) for i in range(lax.axis_size(axi...  4.06 us
    pallas_call x2, Pallas kernels, local(): pl.pallas_call(functools.partial(local_kernel, other), out_shape=shape(NP...  3.77 us
    pallas_call x1, Pallas kernels, per_device(): pl.pallas_call(first_kernel, out_shape=(shape(8, 128), shape(4, 128), sha...  3.17 us
    pallas_call x1, Pallas kernels, per_device(): pl.pallas_call(prep_kernel, out_shape=(half(NZ + 8, LZ),) * 2 + (half(NZ,...  1.12 us
    pallas_call x1, Pallas kernels, per_device(): pl.pallas_call(final_kernel, out_shape=(shape(NX, NY, NZ), shape(1, VERTS...  1.03 us
  transfers between devices with their start and end apart: 13, of which 3 were waited for; matrix products, arithmetic and copies ran while one was open for 0% of the time, Pallas kernels for 15%

profile of v1, /device:TPU:1, one launch (start us, length us, event | category | flops | bytes accessed | tf_op | source)
XLA Modules:
  0.0 39.7 jit_solution(13934055822373436064)
XLA Ops:
  0.6 3.2 %first.1 = (f32[8,128]{1,0:T(8,128)S(1)}, f32[4,128]{1,0:T(4,128)S(1)}, f32[24,128]{1,0:T(8,128)S(1)}, f32[8,128]{1,0:T(8,128)S(1)}, f32[16,32,128]{2,1,0:T(8,12...) custom-call(f32[16,32,128]{2,1,0:T(8,128)} %r_hbm.1, ...), custom_call_target="tpu_custom_call" | custom-call | flops 3145728 | bytes 6500000 | tf_op jit(solution)/shard_map/first/pallas_call | solution.py:357
  3.8 0.0 copy-start
  3.8 3.3 %collective-permute-start = (f32[8,128]{1,0:T(8,128)S(1)}, f32[8,128]{1,0:T(8,128)S(1)}, u32[]{:S(2)}, u32[]{:S(2)}) collective-permute-start(f32[8,128]{1,0:T(8,128)S(1)} %get-tuple-element.40), channel_id=1, source_target_pairs={{0,32},{32,0},{64,96},{96,64},{128,160},{160,128},{192,224},{224,1... | collective-permute-start | bytes 12296 | tf_op jit(solution)/shard_map/ppermute | solution.py:386
  7.1 0.0 collective-permute-start.1
  7.2 0.8 %collective-permute-done.za_ref = f32[8,128]{1,0:T(8,128)S(1)} collective-permute-done((f32[8,128]{1,0:T(8,128)S(1)}, f32[8,128]{1,0:T(8,128)S(1)}, u32[]{:S(2)}, u32[]{:S(2)}) %collective-permute-start) | collective-permute-done | bytes 4128 | tf_op jit(solution)/shard_map/ppermute | solution.py:386
  8.0 1.8 %collective-permute-start.3 = (f32[24,128]{1,0:T(8,128)S(1)}, f32[24,128]{1,0:T(8,128)S(1)}, u32[]{:S(2)}, u32[]{:S(2)}) collective-permute-start(f32[24,128]{1,0:T(8,128)S(1)} %pad_maximum_fusion.partial_ref), channel_id=1, source_target_pairs={{0,2},{1,3},{2,0},{3,1},{4,6},{5,7},{6,4},{7,5},{8,10},{9,11},{10,... | collective-permute-start | bytes 36872 | tf_op jit(solution)/shard_map/ppermute | solution.py:386
  9.7 1.5 %collective-permute-start.4 = (f32[24,128]{1,0:T(8,128)S(1)}, f32[24,128]{1,0:T(8,128)S(1)}, u32[]{:S(2)}, u32[]{:S(2)}) collective-permute-start(f32[24,128]{1,0:T(8,128)S(1)} %pad_maximum_fusion.partial_ref), channel_id=1, source_target_pairs={{0,3},{1,2},{2,1},{3,0},{4,7},{5,6},{6,5},{7,4},{8,11},{9,10},{10,... | collective-permute-start | bytes 36872 | tf_op jit(solution)/shard_map/ppermute | solution.py:386
  11.2 0.0 collective-permute-done.1.zb_ref
  11.2 0.1 edges.1
  11.3 0.2 collective-permute-start.2
  11.5 1.1 %prep.1 = (bf16[136,160]{1,0:T(8,128)(2,1)S(1)}, bf16[136,160]{1,0:T(8,128)(2,1)S(1)}, bf16[128,160]{1,0:T(8,128)(2,1)S(1)}, bf16[128,160]{1,0:T(8,128)(2,1)S(1)...) custom-call(f32[3,10]{1,0:T(4,128)S(1)} %get-tuple-element.44.lam_re, ...), custom_call_target="tpu_custom_call" | custom-call | flops 1000000000 | bytes 1000000 | tf_op jit(solution)/shard_map/prep/pallas_call | solution.py:418
  12.7 6.3 %collective-permute-start.9 = (f32[40,128]{1,0:T(8,128)S(1)}, f32[40,128]{1,0:T(8,128)S(1)}, u32[]{:S(2)}, u32[]{:S(2)}) collective-permute-start(f32[40,128]{1,0:T(8,128)S(1)} %get-tuple-element.67), channel_id=1, source_target_pairs={{0,31},{1,2},{2,1},{3,4},{4,3},{5,6},{6,5},{7,8},{8,7},{9,10},{10,... | collective-permute-start | bytes 61448 | tf_op jit(solution)/shard_map/ppermute | solution.py:390
  19.0 0.0 collective-permute-done.3
  19.0 0.0 collective-permute-done.4
  19.0 0.0 collective-permute-done.2.face_ref
  19.0 0.1 fusion
  19.1 0.0 collective-permute-start.5
  19.1 1.9 %local.2.near_ref = f32[8,32,128]{2,1,0:T(8,128)S(1)} custom-call(f32[16,32,128]{2,1,0:T(8,128)S(1)} %get-tuple-element.41.r_ref, f32[8,128]{1,0:T(8,128)S(1)} %collective-permute-done.za_ref, f32[4,128]{1,0:T(4,128)S(1)} %collective-permute-done.1.zb_ref, f32[64,128]{1,0:T(8,128)S(1)} %collective-permute-done.2.face_ref, ...), custom_call_target="tpu_custom_call" | custom-call | flops 1000000000 | bytes 1000000 | tf_op jit(solution)/shard_map/local/pallas_call | solution.py:433
  21.0 2.7 %collective-permute-done.5 = f32[24,128]{1,0:T(8,128)S(1)} collective-permute-done((f32[24,128]{1,0:T(8,128)S(1)}, f32[24,128]{1,0:T(8,128)S(1)}, u32[]{:S(2)}, u32[]{:S(2)}) %collective-permute-start.5) | collective-permute-done | bytes 12320 | tf_op jit(solution)/shard_map/ppermute | solution.py:386
  23.7 0.1 select_add_fusion.1
  23.8 0.4 collective-permute-start.7
  24.2 0.8 %collective-permute-start.8 = (f32[24,128]{1,0:T(8,128)S(1)}, f32[24,128]{1,0:T(8,128)S(1)}, u32[]{:S(2)}, u32[]{:S(2)}) collective-permute-start(f32[24,128]{1,0:T(8,128)S(1)} %select_add_fusion.1), channel_id=1, source_target_pairs={{0,24},{1,25},{2,26},{3,27},{4,28},{5,29},{6,30},{7,31},{8,16},{9,... | collective-permute-start | bytes 36872 | tf_op jit(solution)/shard_map/ppermute | solution.py:386
  25.0 1.5 %collective-permute-start.6 = (f32[24,128]{1,0:T(8,128)S(1)}, f32[24,128]{1,0:T(8,128)S(1)}, u32[]{:S(2)}, u32[]{:S(2)}) collective-permute-start(f32[24,128]{1,0:T(8,128)S(1)} %select_add_fusion.1), channel_id=1, source_target_pairs={{0,8},{1,9},{2,10},{3,11},{4,12},{5,13},{6,14},{7,15},{8,0},{9,1},... | collective-permute-start | bytes 36872 | tf_op jit(solution)/shard_map/ppermute | solution.py:386
  26.5 0.0 collective-permute-done.9.face_ref
  26.5 1.9 %local.3.far_ref = f32[8,32,128]{2,1,0:T(8,128)S(1)} custom-call(f32[16,32,128]{2,1,0:T(8,128)S(1)} %get-tuple-element.41.r_ref, f32[8,128]{1,0:T(8,128)S(1)} %collective-permute-done.za_ref, f32[4,128]{1,0:T(4,128)S(1)} %collective-permute-done.1.zb_ref, f32[40,128]{1,0:T(8,128)S(1)} %collective-permute-done.9.face_ref, ...), custom_call_target="tpu_custom_call" | custom-call | flops 1000000000 | bytes 1000000 | tf_op jit(solution)/shard_map/local/pallas_call | solution.py:433
  28.4 0.0 collective-permute-done.7
  28.4 0.0 collective-permute-done.8
  28.4 0.0 collective-permute-done.6
  28.4 0.1 select_add_fusion.alpha_ref
  28.5 5.4 %collective-permute-start.12 = (f32[4,128]{1,0:T(4,128)S(1)}, f32[4,128]{1,0:T(4,128)S(1)}, u32[]{:S(2)}, u32[]{:S(2)}) collective-permute-start(f32[4,128]{1,0:T(4,128)S(1)} %slice.19), channel_id=1, source_target_pairs={{0,224},{32,192},{64,160},{96,128},{128,96},{160,64},{192,32},{224... | collective-permute-start | bytes 6152 | tf_op jit(solution)/shard_map/ppermute | solution.py:386
  33.9 0.0 collective-permute-start.10
  33.9 3.4 %collective-permute-start.11 = (f32[4,128]{1,0:T(4,128)S(1)}, f32[4,128]{1,0:T(4,128)S(1)}, u32[]{:S(2)}, u32[]{:S(2)}) collective-permute-start(f32[4,128]{1,0:T(4,128)S(1)} %slice.19), channel_id=1, source_target_pairs={{0,160},{32,128},{64,224},{96,192},{128,32},{160,0},{192,96},{224,... | collective-permute-start | bytes 6152 | tf_op jit(solution)/shard_map/ppermute | solution.py:386
  37.4 0.0 copy-done
  37.4 0.8 %middle.1.base_ref = f32[512,128]{1,0:T(8,128)S(1)} custom-call(f32[8,128]{1,0:T(8,128)S(1)} %get-tuple-element.38.scale_ref, f32[24,128]{1,0:T(8,128)S(1)} %select_add_fusion.alpha_ref, f32[512,512]{1,0:T(8,128)S(1)} %copy-done, f32[512,3072]{1,0:T(8,128)S(1)} %get-tuple-element.69.q_ref), custom_call_target="tpu_custom_call" | custom-call | flops 3670016 | bytes 7000000 | tf_op jit(solution)/shard_map/middle/pallas_call | solution.py:454
  38.1 0.0 collective-permute-done.12
  38.1 0.0 collective-permute-done.10
  38.1 0.5 %collective-permute-done.11 = f32[4,128]{1,0:T(4,128)S(1)} collective-permute-done((f32[4,128]{1,0:T(4,128)S(1)}, f32[4,128]{1,0:T(4,128)S(1)}, u32[]{:S(2)}, u32[]{:S(2)}) %collective-permute-start.11) | collective-permute-done | bytes 2080 | tf_op jit(solution)/shard_map/ppermute | solution.py:386
  38.6 1.0 %final.1 = (f32[16,32,128]{2,1,0:T(8,128)}, f32[1,512]{1,0:T(1,128)}) custom-call(f32[8,128]{1,0:T(8,128)S(1)} %get-tuple-element.38.scale_ref, f32[4,128]{1,0:T(4,128)S(1)} %add_add_fusion.alpha_ref, f32[512,128]{1,0:T(8,128)S(1)} %middle.1.base_ref, f32[8,32,128]{2,1,0:T(8,128)S(1)} %local.2.near_ref, f32[8,32,128]{2,1,0:T(8,128)S(1)} %local.3.far_ref, ...), custom_call_target="tpu_custom_call" | custom-call | flops 524288 | bytes 1500000 | tf_op jit(solution)/shard_map/final/pallas_call | solution.py:464
  (7 shorter events, 0.0 us)
Async XLA Ops:
  3.8 33.6 %copy-start = (f32[512,512]{1,0:T(8,128)S(1)}, f32[512,512]{1,0:T(8,128)}, u32[]{:S(2)}) copy-start(f32[512,512]{1,0:T(8,128)} %leaf_ref.1) | copy-start | bytes 3145732
  3.8 4.2 %collective-permute-start = (f32[8,128]{1,0:T(8,128)S(1)}, f32[8,128]{1,0:T(8,128)S(1)}, u32[]{:S(2)}, u32[]{:S(2)}) collective-permute-start(f32[8,128]{1,0:T(8,128)S(1)} %get-tuple-element.40), channel_id=1, source_target_pairs={{0,32},{32,0},{64,96},{96,64},{128,160},{160,128},{192,224},{224,1... | collective-permute-start | bytes 12296 | tf_op jit(solution)/shard_map/ppermute | solution.py:386
  7.1 4.1 %collective-permute-start.1 = (f32[4,128]{1,0:T(4,128)S(1)}, f32[4,128]{1,0:T(4,128)S(1)}, u32[]{:S(2)}, u32[]{:S(2)}) collective-permute-start(f32[4,128]{1,0:T(4,128)S(1)} %get-tuple-element.42), channel_id=1, source_target_pairs={{0,224},{32,64},{64,32},{96,128},{128,96},{160,192},{192,160},{224... | collective-permute-start | bytes 6152 | tf_op jit(solution)/shard_map/ppermute | solution.py:390
  8.0 11.0 %collective-permute-start.3 = (f32[24,128]{1,0:T(8,128)S(1)}, f32[24,128]{1,0:T(8,128)S(1)}, u32[]{:S(2)}, u32[]{:S(2)}) collective-permute-start(f32[24,128]{1,0:T(8,128)S(1)} %pad_maximum_fusion.partial_ref), channel_id=1, source_target_pairs={{0,2},{1,3},{2,0},{3,1},{4,6},{5,7},{6,4},{7,5},{8,10},{9,11},{10,... | collective-permute-start | bytes 36872 | tf_op jit(solution)/shard_map/ppermute | solution.py:386
  9.7 9.2 %collective-permute-start.4 = (f32[24,128]{1,0:T(8,128)S(1)}, f32[24,128]{1,0:T(8,128)S(1)}, u32[]{:S(2)}, u32[]{:S(2)}) collective-permute-start(f32[24,128]{1,0:T(8,128)S(1)} %pad_maximum_fusion.partial_ref), channel_id=1, source_target_pairs={{0,3},{1,2},{2,1},{3,0},{4,7},{5,6},{6,5},{7,4},{8,11},{9,10},{10,... | collective-permute-start | bytes 36872 | tf_op jit(solution)/shard_map/ppermute | solution.py:386
  11.3 7.6 %collective-permute-start.2 = (f32[64,128]{1,0:T(8,128)S(1)}, f32[64,128]{1,0:T(8,128)S(1)}, u32[]{:S(2)}, u32[]{:S(2)}) collective-permute-start(f32[64,128]{1,0:T(8,128)S(1)} %get-tuple-element.43), channel_id=1, source_target_pairs={{0,1},{1,0},{2,3},{3,2},{4,5},{5,4},{6,7},{7,6},{8,9},{9,8},{10,11... | collective-permute-start | bytes 98312 | tf_op jit(solution)/shard_map/ppermute | solution.py:386
  12.7 13.8 %collective-permute-start.9 = (f32[40,128]{1,0:T(8,128)S(1)}, f32[40,128]{1,0:T(8,128)S(1)}, u32[]{:S(2)}, u32[]{:S(2)}) collective-permute-start(f32[40,128]{1,0:T(8,128)S(1)} %get-tuple-element.67), channel_id=1, source_target_pairs={{0,31},{1,2},{2,1},{3,4},{4,3},{5,6},{6,5},{7,8},{8,7},{9,10},{10,... | collective-permute-start | bytes 61448 | tf_op jit(solution)/shard_map/ppermute | solution.py:390
  19.1 4.7 %collective-permute-start.5 = (f32[24,128]{1,0:T(8,128)S(1)}, f32[24,128]{1,0:T(8,128)S(1)}, u32[]{:S(2)}, u32[]{:S(2)}) collective-permute-start(f32[24,128]{1,0:T(8,128)S(1)} %fusion), channel_id=1, source_target_pairs={{0,6},{1,7},{2,4},{3,5},{4,2},{5,3},{6,0},{7,1},{8,14},{9,15},{10,... | collective-permute-start | bytes 36872 | tf_op jit(solution)/shard_map/ppermute | solution.py:386
  23.8 4.6 %collective-permute-start.7 = (f32[24,128]{1,0:T(8,128)S(1)}, f32[24,128]{1,0:T(8,128)S(1)}, u32[]{:S(2)}, u32[]{:S(2)}) collective-permute-start(f32[24,128]{1,0:T(8,128)S(1)} %select_add_fusion.1), channel_id=1, source_target_pairs={{0,16},{1,17},{2,18},{3,19},{4,20},{5,21},{6,22},{7,23},{8,24},{9,... | collective-permute-start | bytes 36872 | tf_op jit(solution)/shard_map/ppermute | solution.py:386
  24.2 4.2 %collective-permute-start.8 = (f32[24,128]{1,0:T(8,128)S(1)}, f32[24,128]{1,0:T(8,128)S(1)}, u32[]{:S(2)}, u32[]{:S(2)}) collective-permute-start(f32[24,128]{1,0:T(8,128)S(1)} %select_add_fusion.1), channel_id=1, source_target_pairs={{0,24},{1,25},{2,26},{3,27},{4,28},{5,29},{6,30},{7,31},{8,16},{9,... | collective-permute-start | bytes 36872 | tf_op jit(solution)/shard_map/ppermute | solution.py:386
  25.0 3.4 %collective-permute-start.6 = (f32[24,128]{1,0:T(8,128)S(1)}, f32[24,128]{1,0:T(8,128)S(1)}, u32[]{:S(2)}, u32[]{:S(2)}) collective-permute-start(f32[24,128]{1,0:T(8,128)S(1)} %select_add_fusion.1), channel_id=1, source_target_pairs={{0,8},{1,9},{2,10},{3,11},{4,12},{5,13},{6,14},{7,15},{8,0},{9,1},... | collective-permute-start | bytes 36872 | tf_op jit(solution)/shard_map/ppermute | solution.py:386
  28.5 9.6 %collective-permute-start.12 = (f32[4,128]{1,0:T(4,128)S(1)}, f32[4,128]{1,0:T(4,128)S(1)}, u32[]{:S(2)}, u32[]{:S(2)}) collective-permute-start(f32[4,128]{1,0:T(4,128)S(1)} %slice.19), channel_id=1, source_target_pairs={{0,224},{32,192},{64,160},{96,128},{128,96},{160,64},{192,32},{224... | collective-permute-start | bytes 6152 | tf_op jit(solution)/shard_map/ppermute | solution.py:386
  33.9 4.2 %collective-permute-start.10 = (f32[4,128]{1,0:T(4,128)S(1)}, f32[4,128]{1,0:T(4,128)S(1)}, u32[]{:S(2)}, u32[]{:S(2)}) collective-permute-start(f32[4,128]{1,0:T(4,128)S(1)} %slice.19), channel_id=1, source_target_pairs={{0,96},{32,64},{64,32},{96,0},{128,224},{160,192},{192,160},{224,1... | collective-permute-start | bytes 6152 | tf_op jit(solution)/shard_map/ppermute | solution.py:386
  33.9 4.7 %collective-permute-start.11 = (f32[4,128]{1,0:T(4,128)S(1)}, f32[4,128]{1,0:T(4,128)S(1)}, u32[]{:S(2)}, u32[]{:S(2)}) collective-permute-start(f32[4,128]{1,0:T(4,128)S(1)} %slice.19), channel_id=1, source_target_pairs={{0,160},{32,128},{64,224},{96,192},{128,32},{160,0},{192,96},{224,... | collective-permute-start | bytes 6152 | tf_op jit(solution)/shard_map/ppermute | solution.py:386

commit v2 on v1

--- a/solution.py
+++ b/solution.py
@@ -99,6 +99,7 @@
 FACE = NY + 8
 PARTIALS = LEVELS * TILES
 LAST = PARTIALS - TILES
+SUMS = 2 * LAST + TILES
 
 
 def first_kernel(
@@ -166,13 +167,20 @@
     for t in range(PARTIALS):
         total = jnp.sum(acc[t], axis=0, keepdims=True) * scales[t // TILES]
         out_ref[t : t + 1, :] = total
-        if t >= LAST:
-            face_a_ref[4 + t - LAST : 5 + t - LAST, :] = total
+        face_a_ref[8 + t : 9 + t, :] = total
     for copy in small[3:]:
         copy.wait()
 
 
-def edge_kernel(r_ref, za_ref, zb_ref, partial_ref, a_ref, b_ref):
+def join_kernel(partial_ref, za_ref, out_ref):
+    side = odd("gz") == 1
+    mine, other = partial_ref[...], za_ref[8 : 8 + PARTIALS, :]
+    out_ref[0:LAST, :] = jnp.where(side, other, mine)[0:LAST]
+    out_ref[LAST : 2 * LAST, :] = jnp.where(side, mine, other)[0:LAST]
+    out_ref[2 * LAST : SUMS, :] = (mine + other)[LAST:]
+
+
+def edge_kernel(r_ref, za_ref, zb_ref, sums_ref, a_ref, b_ref):
     side = odd("gz")
     za, zb = za_ref[0:4, :], inside("gz", zb_ref[...])
     low = jnp.where(side == 1, za, zb)
@@ -184,10 +192,18 @@
         out[NY:FACE, :] = jnp.zeros((8, NZ), F32)
         for i, edge in enumerate((low, high)):
             out[NY + i : NY + i + 1, 0:NY] = jnp.where(take, edge[0:1, 0:NY], edge[3:4, 128 - NY :])
-    a_ref[FACE : FACE + PARTIALS, :] = partial_ref[...]
-
-
-def middle_kernel(scale_ref, alpha_ref, leaf_ref, q_ref, out_ref):
+    a_ref[FACE : FACE + SUMS, :] = sums_ref[...]
+
+
+def middle_kernel(
+    scale_ref, alpha_ref, leaf_ref, q_ref, near_ref, far_ref, in0_ref, in1_ref, out_ref, local_ref
+):
+    before = odd("xy") == 1
+    near, far = near_ref[...], far_ref[...]
+    bz_in = (in0_ref[...], in1_ref[...])
+    for a, inner in enumerate((jnp.where(before, near, far), jnp.where(before, far, near))):
+        result = dot3(split(inner), bz_in, NT)
+        local_ref[a * NP : (a + 1) * NP] = result.reshape(NP, NY, NZ)
     acc = [jnp.zeros((8, 128), F32) for _ in range(TILES)]
     values = vertex_values(scale_ref[LEVELS : LEVELS + 1, :], scale_ref[LEVELS + 1 : LEVELS + 2, :])
     for g, b in enumerate(values):
@@ -195,9 +211,11 @@
             acc[t] = acc[t] + leaf_ref[g * 8 : g * 8 + 8, t * 128 : (t + 1) * 128] * b
     leaf_alpha = [jnp.sum(acc[t], axis=0, keepdims=True) for t in range(TILES)]
     alpha = []
+    side = odd("gz") == 1
     for t in range((LEVELS - 1) * TILES):
         level = t // TILES
-        alpha.append(alpha_ref[t : t + 1, :] * scale_ref[level : level + 1, :])
+        row = jnp.where(side, alpha_ref[LAST + t : LAST + t + 1, :], alpha_ref[t : t + 1, :])
+        alpha.append(row * scale_ref[level : level + 1, :])
     for c in range(CHUNKS):
         rows = slice(c * ROWS, (c + 1) * ROWS)
         total = leaf_ref[rows, 0:128] * leaf_alpha[0]
@@ -208,7 +226,7 @@
         out_ref[rows, :] = total
 
 
-def final_kernel(scale_ref, alpha_ref, base_ref, near_ref, far_ref, q_ref, out_ref, sol_ref):
+def final_kernel(scale_ref, alpha_ref, base_ref, local_ref, q_ref, out_ref, sol_ref):
     alpha = alpha_ref[...] * scale_ref[LEVELS - 1 : LEVELS, :]
     start = (LEVELS - 1) * SW
     vm_row = scale_ref[LEVELS : LEVELS + 1, :]
@@ -228,12 +246,10 @@
     mine = (iota((8, ELEMS), 1) >> 4) == iota((8, ELEMS), 0)
     spread = mark((iota((ELEMS, NZ), 0) & (EZ - 1)) == (iota((ELEMS, NZ), 1) >> 3))
     rows = dot_onehot(jnp.where(mine, per_element, 0.0), spread)
-    turned = odd("xy") == 1
     for a in range(EX):
         add = jnp.broadcast_to(rows[a * EY : (a + 1) * EY, None, :], (EY, NP, NZ)).reshape(NY, NZ)
         for i in range(NP):
-            local = jnp.where(turned == (a == 0), near_ref[i], far_ref[i])
-            out_ref[a * NP + i] = local + add
+            out_ref[a * NP + i] = local_ref[a * NP + i] + add
     ones = jnp.ones((8, 128), BF16)
     row = [bdot(ones, part.astype(BF16), NT) for part in split3(jnp.concatenate(totals, axis=0))]
     sol_ref[...] = (row[0] + (row[1] + row[2]))[0:1]
@@ -301,7 +317,7 @@
 
 def local_kernel(
     other, r_ref, za_ref, zb_ref, face_ref,
-    bz0_ref, bz1_ref, in0_ref, in1_ref, f0_ref, f1_ref, k0_ref, k1_ref, inv_ref, out_ref,
+    bz0_ref, bz1_ref, f0_ref, f1_ref, k0_ref, k1_ref, inv_ref, out_ref,
 ):
     row = iota((8, 128), 0)
     side = odd("gz")
@@ -331,9 +347,7 @@
     points = jnp.concatenate([points, sides], axis=1)
     window = split(dot3(split(points), (bz0_ref[...], bz1_ref[...])))
     scaled = dot3((f0_ref[...], f1_ref[...]), window) * inv_ref[at]
-    inner = dot3((k0_ref[...], k1_ref[...]), split(scaled))
-    result = dot3(split(inner), (in0_ref[...], in1_ref[...]), NT)
-    out_ref[...] = result.reshape(NP, NY, NZ)
+    out_ref[...] = dot3((k0_ref[...], k1_ref[...]), split(scaled))
 
 
 def shape(*dims):
@@ -357,7 +371,7 @@
     face_a, face_b, partial, aux, points, separators, vectors, values, scale = pl.pallas_call(
         first_kernel,
         out_shape=(
-            shape(8, 128), shape(4, 128), shape(PARTIALS, 128), shape(8, 128),
+            shape(8 + PARTIALS, 128), shape(4, 128), shape(PARTIALS, 128), shape(8, 128),
             shape(NX, NY, NZ), shape(VERTS, LEVELS * SW),
             shape(PTS, 3, PTS), shape(3, PTS), shape(EX, EY, EZ),
         ),
@@ -392,12 +406,19 @@
     z_a = swap(face_a, "gz", 1)
     z_b = pairs(face_b, "gz")
 
-    last = partial[LAST:] + z_a[4:]
-    total = jnp.concatenate([partial[:LAST], last], axis=0)
+    total = pl.pallas_call(
+        join_kernel,
+        out_shape=shape(SUMS, 128),
+        in_specs=[VMEM] * 2,
+        out_specs=VMEM,
+        compiler_params=PARAMS,
+        cost_estimate=cost(1000, 50_000),
+        name="join",
+    )(partial, z_a)
 
     message_a, message_b = pl.pallas_call(
         edge_kernel,
-        out_shape=(shape(FACE + PARTIALS, NZ), shape(FACE, NZ)),
+        out_shape=(shape(FACE + SUMS, NZ), shape(FACE, NZ)),
         in_specs=[VMEM] * 4,
         out_specs=(VMEM, VMEM),
         compiler_params=PARAMS,
@@ -405,14 +426,19 @@
         name="edges",
     )(points, z_a, z_b, total)
 
-    level = jnp.arange(PARTIALS, dtype=jnp.int32)[:, None] // TILES
+    row = jnp.arange(SUMS, dtype=jnp.int32)[:, None]
+    level = jnp.where(row < 2 * LAST, row % LAST, LAST) // TILES
 
     def from_level(value, first):
         return jnp.where(level >= first, value, 0.0)
 
-    two, three = swap(total, "xy", 2), swap(total, "xy", 3)
+    def cross(value, bits):
+        count = lax.axis_size("gz") * lax.axis_size("xy")
+        partner = lax.axis_size("xy") ^ bits
+        return lax.ppermute(value, ("gz", "xy"), [(i, i ^ partner) for i in range(count)])
+
+    two, three = cross(total, 2), cross(total, 3)
     x_a = swap(message_a, "xy", 1)
-    x_b = pairs(message_b, "xy")
     total = total + x_a[FACE:] + from_level(two + three, 1)
     half = lambda *dims: jax.ShapeDtypeStruct(dims, BF16)
     matrices = pl.pallas_call(
@@ -432,44 +458,45 @@
     def local(other, face):
         return pl.pallas_call(
             functools.partial(local_kernel, other),
-            out_shape=shape(NP, NY, NZ),
-            in_specs=[VMEM] * 13,
+            out_shape=shape(NP * NY, LZ),
+            in_specs=[VMEM] * 11,
             out_specs=VMEM,
             compiler_params=PARAMS,
             cost_estimate=cost(1_000_000_000, 1_000_000),
             name="local",
-        )(points, z_a, z_b, face, *matrices)
-
-    total, matrices = lax.optimization_barrier((total, matrices))
+        )(points, z_a, z_b, face, *matrices[:2], *matrices[4:])
+
+    total, matrices, message_b = lax.optimization_barrier((total, matrices, message_b))
+    x_b = pairs(message_b, "xy")
     near = local(False, x_a)
-    total = total + from_level(swap(total, "xy", 6), 2)
+    total = total + from_level(cross(total, 6), 2)
     total, near = lax.optimization_barrier((total, near))
     far = local(True, x_b)
-    one, two, three = (swap(total, "xy", bits) for bits in (8, 16, 24))
+    one, two, three = (cross(total, bits) for bits in (8, 16, 24))
     total = total + from_level(one, 3) + from_level(two + three, 4)
     total, far = lax.optimization_barrier((total, far))
-    last = total[LAST:]
-    last = last + (swap(last, "gz", 3) + swap(last, "gz", 5) + swap(last, "gz", 7))
-
-    base = pl.pallas_call(
+    last = total[2 * LAST :]
+    last = last + (swap(last, "gz", 7) + swap(last, "gz", 3) + swap(last, "gz", 5))
+
+    base, local = pl.pallas_call(
         middle_kernel,
-        out_shape=shape(VERTS, 128),
-        in_specs=[VMEM] * 4,
-        out_specs=VMEM,
+        out_shape=(shape(VERTS, 128), shape(NX, NY, NZ)),
+        in_specs=[VMEM] * 8,
+        out_specs=(VMEM, VMEM),
         compiler_params=PARAMS,
         cost_estimate=cost(7 * 512 * 512 * 2, 7_000_000),
         name="middle",
-    )(aux, total, leaf_columns, separators)
+    )(aux, total, leaf_columns, separators, near, far, matrices[2], matrices[3])
 
     out, sol = pl.pallas_call(
         final_kernel,
         out_shape=(shape(NX, NY, NZ), shape(1, VERTS)),
-        in_specs=[VMEM] * 6,
+        in_specs=[VMEM] * 5,
         out_specs=(VMEM, VMEM),
         compiler_params=PARAMS,
         cost_estimate=cost(512 * 512 * 2, 1_500_000),
         name="final",
-    )(aux, last, base, near, far, separators)
+    )(aux, last, base, local, separators)
     return out, sol.reshape(VERTS)
 
 

time: 39.8 us -> 38 us (0.955)
  starting transfers between devices: 24.6 us -> 21.9 us
  waiting for transfers between devices: 4.06 us -> 5.05 us
    ppermute x0 -> x6, starting transfers between devices: none -> 13.4 us  [cross(): lax.ppermute(value, ('gz', 'xy'), [(i, i ^ partner) for i in range(count)])]
    ppermute x11 -> x5, starting transfers between devices: 18.3 us -> 6.58 us  [swap(): lax.ppermute(value, axis, [(i, i ^ bits) for i in range(lax.axis_size(axi...]
    ppermute x2, starting transfers between devices: 6.3 us -> 1.94 us  [pairs(): lax.ppermute(value, axis, [(i, (i + 2 * (i % 2) - 1) % count) for i in ra...]
    ppermute x0 -> x6, waiting for transfers between devices: none -> 2.39 us  [cross(): lax.ppermute(value, ('gz', 'xy'), [(i, i ^ partner) for i in range(count)])]
    ppermute x11 -> x5, waiting for transfers between devices: 4.06 us -> 2.65 us  [swap(): lax.ppermute(value, axis, [(i, i ^ bits) for i in range(lax.axis_size(axi...]
    pallas_call x3 -> x4, Pallas kernels: 4.07 us -> 4.32 us  [the longest x1 3.17 us: per_device(): pl.pallas_call(first_kernel, out_shape=(shape(8 + PARTIALS, 128), shape(4...]
  transfers between devices with their start and end apart: 13 -> 13, of which waited for: 3 -> 5; matrix products, arithmetic and copies ran while one was open for 0% -> 0% of each run, Pallas kernels for 15% -> 15%
where the time goes in v2:
time: 38 us; the launch traced here: 37.9 us
  starting transfers between devices  21.9 us (58%)
  Pallas kernels  9.86 us (26%)
  waiting for transfers between devices  5.05 us (13%)
  between operations  0.74 us (2%)
    ppermute x6, starting transfers between devices, cross(): lax.ppermute(value, ('gz', 'xy'), [(i, i ^ partner) for i in range(count)])  13.4 us
    ppermute x5, starting transfers between devices, swap(): lax.ppermute(value, axis, [(i, i ^ bits) for i in range(lax.axis_size(axi...  6.58 us
    pallas_call x2, Pallas kernels, local(): pl.pallas_call(functools.partial(local_kernel, other), out_shape=shape(NP...  3.41 us
    pallas_call x1, Pallas kernels, per_device(): pl.pallas_call(first_kernel, out_shape=(shape(8 + PARTIALS, 128), shape(4...  3.17 us
    ppermute x5, waiting for transfers between devices, swap(): lax.ppermute(value, axis, [(i, i ^ bits) for i in range(lax.axis_size(axi...  2.65 us
    ppermute x6, waiting for transfers between devices, cross(): lax.ppermute(value, ('gz', 'xy'), [(i, i ^ partner) for i in range(count)])  2.39 us
    ppermute x2, starting transfers between devices, pairs(): lax.ppermute(value, axis, [(i, (i + 2 * (i % 2) - 1) % count) for i in ra...  1.94 us
    pallas_call x1, Pallas kernels, per_device(): pl.pallas_call(prep_kernel, out_shape=(half(NZ + 8, LZ),) * 2 + (half(NZ,...  1.12 us
  transfers between devices with their start and end apart: 13, of which 5 were waited for; matrix products, arithmetic and copies ran while one was open for 0% of the time, Pallas kernels for 15%

profile of v2, /device:TPU:1, one launch (start us, length us, event | category | flops | bytes accessed | tf_op | source)
XLA Modules:
  0.0 37.9 jit_solution(4023263116113966047)
XLA Ops:
  0.6 3.2 %first.1 = (f32[32,128]{1,0:T(8,128)S(1)}, f32[4,128]{1,0:T(4,128)S(1)}, f32[24,128]{1,0:T(8,128)S(1)}, f32[8,128]{1,0:T(8,128)S(1)}, f32[16,32,128]{2,1,0:T(8,1...) custom-call(f32[16,32,128]{2,1,0:T(8,128)} %r_hbm.1, ...), custom_call_target="tpu_custom_call" | custom-call | flops 3145728 | bytes 6500000 | tf_op jit(solution)/shard_map/first/pallas_call | solution.py:371
  3.8 0.0 copy-start
  3.8 3.3 %collective-permute-start = (f32[32,128]{1,0:T(8,128)S(1)}, f32[32,128]{1,0:T(8,128)S(1)}, u32[]{:S(2)}, u32[]{:S(2)}) collective-permute-start(f32[32,128]{1,0:T(8,128)S(1)} %get-tuple-element.43), channel_id=1, source_target_pairs={{0,32},{32,0},{64,96},{96,64},{128,160},{160,128},{192,224},{224,1... | collective-permute-start | bytes 49160 | tf_op jit(solution)/shard_map/ppermute | solution.py:400
  7.2 0.0 collective-permute-start.1
  7.2 0.8 %collective-permute-done.za_ref = f32[32,128]{1,0:T(8,128)S(1)} collective-permute-done((f32[32,128]{1,0:T(8,128)S(1)}, f32[32,128]{1,0:T(8,128)S(1)}, u32[]{:S(2)}, u32[]{:S(2)}) %collective-permute-start) | collective-permute-done | bytes 16416 | tf_op jit(solution)/shard_map/ppermute | solution.py:400
  8.0 3.4 %collective-permute-start.3 = (f32[44,128]{1,0:T(8,128)S(1)}, f32[44,128]{1,0:T(8,128)S(1)}, u32[]{:S(2)}, u32[]{:S(2)}) collective-permute-start(f32[44,128]{1,0:T(8,128)S(1)} %join.1.sums_ref), channel_id=1, source_target_pairs={{0,34},{1,35},{2,32},{3,33},{4,38},{5,39},{6,36},{7,37},{8,42},{9,... | collective-permute-start | bytes 67592 | tf_op jit(solution)/shard_map/ppermute | solution.py:438
  11.4 1.5 %collective-permute-start.4 = (f32[44,128]{1,0:T(8,128)S(1)}, f32[44,128]{1,0:T(8,128)S(1)}, u32[]{:S(2)}, u32[]{:S(2)}) collective-permute-start(f32[44,128]{1,0:T(8,128)S(1)} %join.1.sums_ref), channel_id=1, source_target_pairs={{0,35},{1,34},{2,33},{3,32},{4,39},{5,38},{6,37},{7,36},{8,43},{9,... | collective-permute-start | bytes 67592 | tf_op jit(solution)/shard_map/ppermute | solution.py:438
  12.8 0.0 collective-permute-done.1.zb_ref
  12.8 0.1 edges.1
  13.0 0.2 collective-permute-start.2
  13.1 1.1 %prep.1 = (bf16[136,160]{1,0:T(8,128)(2,1)S(1)}, bf16[136,160]{1,0:T(8,128)(2,1)S(1)}, bf16[128,160]{1,0:T(8,128)(2,1)S(1)}, bf16[128,160]{1,0:T(8,128)(2,1)S(1)...) custom-call(f32[3,10]{1,0:T(4,128)S(1)} %get-tuple-element.47.lam_re, ...), custom_call_target="tpu_custom_call" | custom-call | flops 1000000000 | bytes 1000000 | tf_op jit(solution)/shard_map/prep/pallas_call | solution.py:444
  14.3 0.0 collective-permute-done.3
  14.3 2.2 %collective-permute-done.4 = f32[44,128]{1,0:T(8,128)S(1)} collective-permute-done((f32[44,128]{1,0:T(8,128)S(1)}, f32[44,128]{1,0:T(8,128)S(1)}, u32[]{:S(2)}, u32[]{:S(2)}) %collective-permute-start.4) | collective-permute-done | bytes 22560 | tf_op jit(solution)/shard_map/ppermute | solution.py:438
  16.5 0.0 collective-permute-done.2.face_ref
  16.5 0.1 fusion
  16.6 4.3 %collective-permute-start.5 = (f32[44,128]{1,0:T(8,128)S(1)}, f32[44,128]{1,0:T(8,128)S(1)}, u32[]{:S(2)}, u32[]{:S(2)}) collective-permute-start(f32[44,128]{1,0:T(8,128)S(1)} %fusion), channel_id=1, source_target_pairs={{0,38},{1,39},{2,36},{3,37},{4,34},{5,35},{6,32},{7,33},{8,46},{9,... | collective-permute-start | bytes 67592 | tf_op jit(solution)/shard_map/ppermute | solution.py:438
  20.9 1.9 %collective-permute-start.9 = (f32[40,128]{1,0:T(8,128)S(1)}, f32[40,128]{1,0:T(8,128)S(1)}, u32[]{:S(2)}, u32[]{:S(2)}) collective-permute-start(f32[40,128]{1,0:T(8,128)S(1)} %get-tuple-element.69), channel_id=1, source_target_pairs={{0,31},{1,2},{2,1},{3,4},{4,3},{5,6},{6,5},{7,8},{8,7},{9,10},{10,... | collective-permute-start | bytes 61448 | tf_op jit(solution)/shard_map/ppermute | solution.py:404
  22.8 1.7 %local.2.near_ref = f32[256,160]{1,0:T(8,128)S(1)} custom-call(f32[16,32,128]{2,1,0:T(8,128)S(1)} %get-tuple-element.44.r_ref, f32[32,128]{1,0:T(8,128)S(1)} %collective-permute-done.za_ref, f32[4,128]{1,0:T(4,128)S(1)} %collective-permute-done.1.zb_ref, f32[84,128]{1,0:T(8,128)S(1)} %collective-permute-done.2.face_ref, ...), custom_call_target="tpu_custom_call" | custom-call | flops 1000000000 | bytes 1000000 | tf_op jit(solution)/shard_map/local/pallas_call | solution.py:459
  24.5 0.0 collective-permute-done.5
  24.5 0.1 select_add_fusion.1
  24.6 1.7 %collective-permute-start.7 = (f32[44,128]{1,0:T(8,128)S(1)}, f32[44,128]{1,0:T(8,128)S(1)}, u32[]{:S(2)}, u32[]{:S(2)}) collective-permute-start(f32[44,128]{1,0:T(8,128)S(1)} %select_add_fusion.1), channel_id=1, source_target_pairs={{0,48},{1,49},{2,50},{3,51},{4,52},{5,53},{6,54},{7,55},{8,56},{9,... | collective-permute-start | bytes 67592 | tf_op jit(solution)/shard_map/ppermute | solution.py:438
  26.3 0.3 collective-permute-start.8
  26.7 2.2 %collective-permute-start.6 = (f32[44,128]{1,0:T(8,128)S(1)}, f32[44,128]{1,0:T(8,128)S(1)}, u32[]{:S(2)}, u32[]{:S(2)}) collective-permute-start(f32[44,128]{1,0:T(8,128)S(1)} %select_add_fusion.1), channel_id=1, source_target_pairs={{0,40},{1,41},{2,42},{3,43},{4,44},{5,45},{6,46},{7,47},{8,32},{9,... | collective-permute-start | bytes 67592 | tf_op jit(solution)/shard_map/ppermute | solution.py:438
  28.9 0.0 collective-permute-done.9.face_ref
  28.9 1.7 %local.3.far_ref = f32[256,160]{1,0:T(8,128)S(1)} custom-call(f32[16,32,128]{2,1,0:T(8,128)S(1)} %get-tuple-element.44.r_ref, f32[32,128]{1,0:T(8,128)S(1)} %collective-permute-done.za_ref, f32[4,128]{1,0:T(4,128)S(1)} %collective-permute-done.1.zb_ref, f32[40,128]{1,0:T(8,128)S(1)} %collective-permute-done.9.face_ref, ...), custom_call_target="tpu_custom_call" | custom-call | flops 1000000000 | bytes 1000000 | tf_op jit(solution)/shard_map/local/pallas_call | solution.py:459
  30.6 0.0 collective-permute-done.7
  30.6 0.2 collective-permute-done.8
  30.8 0.0 collective-permute-done.6
  30.8 0.1 select_add_fusion.alpha_ref
  30.9 1.7 %collective-permute-start.12 = (f32[4,128]{1,0:T(4,128)S(1)}, f32[4,128]{1,0:T(4,128)S(1)}, u32[]{:S(2)}, u32[]{:S(2)}) collective-permute-start(f32[4,128]{1,0:T(4,128)S(1)} %slice.7), channel_id=1, source_target_pairs={{0,160},{32,128},{64,224},{96,192},{128,32},{160,0},{192,96},{224,... | collective-permute-start | bytes 6152 | tf_op jit(solution)/shard_map/ppermute | solution.py:400
  32.6 1.1 %collective-permute-start.10 = (f32[4,128]{1,0:T(4,128)S(1)}, f32[4,128]{1,0:T(4,128)S(1)}, u32[]{:S(2)}, u32[]{:S(2)}) collective-permute-start(f32[4,128]{1,0:T(4,128)S(1)} %slice.7), channel_id=1, source_target_pairs={{0,224},{32,192},{64,160},{96,128},{128,96},{160,64},{192,32},{224... | collective-permute-start | bytes 6152 | tf_op jit(solution)/shard_map/ppermute | solution.py:400
  33.7 0.2 collective-permute-start.11
  34.0 0.0 copy-done
  34.0 1.0 %middle.1 = (f32[512,128]{1,0:T(8,128)S(1)}, f32[16,32,128]{2,1,0:T(8,128)S(1)}) custom-call(f32[8,128]{1,0:T(8,128)S(1)} %get-tuple-element.41.scale_ref, f32[44,128]{1,0:T(8,128)S(1)} %select_add_fusion.alpha_ref, f32[512,512]{1,0:T(8,128)S(1)} %copy-done, f32[512,3072]{1,0:T(8,128)S(1)} %get-tuple-element.71.q_ref, f32[256,160]{1,0:T(8,128)S(1)} %local.2.near_ref, ...), custom_call_target="tpu_custom_call" | custom-call | flops 3670016 | bytes 7000000 | tf_op jit(solution)/shard_map/middle/pallas_call | solution.py:481
  35.0 0.5 %collective-permute-done.12 = f32[4,128]{1,0:T(4,128)S(1)} collective-permute-done((f32[4,128]{1,0:T(4,128)S(1)}, f32[4,128]{1,0:T(4,128)S(1)}, u32[]{:S(2)}, u32[]{:S(2)}) %collective-permute-start.12) | collective-permute-done | bytes 2080 | tf_op jit(solution)/shard_map/ppermute | solution.py:400
  35.5 1.3 %collective-permute-done.10 = f32[4,128]{1,0:T(4,128)S(1)} collective-permute-done((f32[4,128]{1,0:T(4,128)S(1)}, f32[4,128]{1,0:T(4,128)S(1)}, u32[]{:S(2)}, u32[]{:S(2)}) %collective-permute-start.10) | collective-permute-done | bytes 2080 | tf_op jit(solution)/shard_map/ppermute | solution.py:400
  36.8 0.0 collective-permute-done.11
  36.8 1.0 %final.1 = (f32[16,32,128]{2,1,0:T(8,128)}, f32[1,512]{1,0:T(1,128)}) custom-call(f32[8,128]{1,0:T(8,128)S(1)} %get-tuple-element.41.scale_ref, f32[4,128]{1,0:T(4,128)S(1)} %add_add_fusion.alpha_ref, f32[512,128]{1,0:T(8,128)S(1)} %get-tuple-element.76.base_ref, f32[16,32,128]{2,1,0:T(8,128)S(1)} %get-tuple-element.77.local_ref, ...), custom_call_target="tpu_custom_call" | custom-call | flops 524288 | bytes 1500000 | tf_op jit(solution)/shard_map/final/pallas_call | solution.py:491
  (6 shorter events, 0.1 us)
Async XLA Ops:
  3.8 30.2 %copy-start = (f32[512,512]{1,0:T(8,128)S(1)}, f32[512,512]{1,0:T(8,128)}, u32[]{:S(2)}) copy-start(f32[512,512]{1,0:T(8,128)} %leaf_ref.1) | copy-start | bytes 3145732
  3.8 4.2 %collective-permute-start = (f32[32,128]{1,0:T(8,128)S(1)}, f32[32,128]{1,0:T(8,128)S(1)}, u32[]{:S(2)}, u32[]{:S(2)}) collective-permute-start(f32[32,128]{1,0:T(8,128)S(1)} %get-tuple-element.43), channel_id=1, source_target_pairs={{0,32},{32,0},{64,96},{96,64},{128,160},{160,128},{192,224},{224,1... | collective-permute-start | bytes 49160 | tf_op jit(solution)/shard_map/ppermute | solution.py:400
  7.2 5.7 %collective-permute-start.1 = (f32[4,128]{1,0:T(4,128)S(1)}, f32[4,128]{1,0:T(4,128)S(1)}, u32[]{:S(2)}, u32[]{:S(2)}) collective-permute-start(f32[4,128]{1,0:T(4,128)S(1)} %get-tuple-element.45), channel_id=1, source_target_pairs={{0,224},{32,64},{64,32},{96,128},{128,96},{160,192},{192,160},{224... | collective-permute-start | bytes 6152 | tf_op jit(solution)/shard_map/ppermute | solution.py:404
  8.0 6.3 %collective-permute-start.3 = (f32[44,128]{1,0:T(8,128)S(1)}, f32[44,128]{1,0:T(8,128)S(1)}, u32[]{:S(2)}, u32[]{:S(2)}) collective-permute-start(f32[44,128]{1,0:T(8,128)S(1)} %join.1.sums_ref), channel_id=1, source_target_pairs={{0,34},{1,35},{2,32},{3,33},{4,38},{5,39},{6,36},{7,37},{8,42},{9,... | collective-permute-start | bytes 67592 | tf_op jit(solution)/shard_map/ppermute | solution.py:438
  11.4 5.2 %collective-permute-start.4 = (f32[44,128]{1,0:T(8,128)S(1)}, f32[44,128]{1,0:T(8,128)S(1)}, u32[]{:S(2)}, u32[]{:S(2)}) collective-permute-start(f32[44,128]{1,0:T(8,128)S(1)} %join.1.sums_ref), channel_id=1, source_target_pairs={{0,35},{1,34},{2,33},{3,32},{4,39},{5,38},{6,37},{7,36},{8,43},{9,... | collective-permute-start | bytes 67592 | tf_op jit(solution)/shard_map/ppermute | solution.py:438
  13.0 3.6 %collective-permute-start.2 = (f32[84,128]{1,0:T(8,128)S(1)}, f32[84,128]{1,0:T(8,128)S(1)}, u32[]{:S(2)}, u32[]{:S(2)}) collective-permute-start(f32[84,128]{1,0:T(8,128)S(1)} %get-tuple-element.46), channel_id=1, source_target_pairs={{0,1},{1,0},{2,3},{3,2},{4,5},{5,4},{6,7},{7,6},{8,9},{9,8},{10,11... | collective-permute-start | bytes 129032 | tf_op jit(solution)/shard_map/ppermute | solution.py:400
  16.6 7.9 %collective-permute-start.5 = (f32[44,128]{1,0:T(8,128)S(1)}, f32[44,128]{1,0:T(8,128)S(1)}, u32[]{:S(2)}, u32[]{:S(2)}) collective-permute-start(f32[44,128]{1,0:T(8,128)S(1)} %fusion), channel_id=1, source_target_pairs={{0,38},{1,39},{2,36},{3,37},{4,34},{5,35},{6,32},{7,33},{8,46},{9,... | collective-permute-start | bytes 67592 | tf_op jit(solution)/shard_map/ppermute | solution.py:438
  20.9 8.0 %collective-permute-start.9 = (f32[40,128]{1,0:T(8,128)S(1)}, f32[40,128]{1,0:T(8,128)S(1)}, u32[]{:S(2)}, u32[]{:S(2)}) collective-permute-start(f32[40,128]{1,0:T(8,128)S(1)} %get-tuple-element.69), channel_id=1, source_target_pairs={{0,31},{1,2},{2,1},{3,4},{4,3},{5,6},{6,5},{7,8},{8,7},{9,10},{10,... | collective-permute-start | bytes 61448 | tf_op jit(solution)/shard_map/ppermute | solution.py:404
  24.6 6.0 %collective-permute-start.7 = (f32[44,128]{1,0:T(8,128)S(1)}, f32[44,128]{1,0:T(8,128)S(1)}, u32[]{:S(2)}, u32[]{:S(2)}) collective-permute-start(f32[44,128]{1,0:T(8,128)S(1)} %select_add_fusion.1), channel_id=1, source_target_pairs={{0,48},{1,49},{2,50},{3,51},{4,52},{5,53},{6,54},{7,55},{8,56},{9,... | collective-permute-start | bytes 67592 | tf_op jit(solution)/shard_map/ppermute | solution.py:438
  26.3 4.5 %collective-permute-start.8 = (f32[44,128]{1,0:T(8,128)S(1)}, f32[44,128]{1,0:T(8,128)S(1)}, u32[]{:S(2)}, u32[]{:S(2)}) collective-permute-start(f32[44,128]{1,0:T(8,128)S(1)} %select_add_fusion.1), channel_id=1, source_target_pairs={{0,56},{1,57},{2,58},{3,59},{4,60},{5,61},{6,62},{7,63},{8,48},{9,... | collective-permute-start | bytes 67592 | tf_op jit(solution)/shard_map/ppermute | solution.py:438
  26.7 4.1 %collective-permute-start.6 = (f32[44,128]{1,0:T(8,128)S(1)}, f32[44,128]{1,0:T(8,128)S(1)}, u32[]{:S(2)}, u32[]{:S(2)}) collective-permute-start(f32[44,128]{1,0:T(8,128)S(1)} %select_add_fusion.1), channel_id=1, source_target_pairs={{0,40},{1,41},{2,42},{3,43},{4,44},{5,45},{6,46},{7,47},{8,32},{9,... | collective-permute-start | bytes 67592 | tf_op jit(solution)/shard_map/ppermute | solution.py:438
  30.9 4.6 %collective-permute-start.12 = (f32[4,128]{1,0:T(4,128)S(1)}, f32[4,128]{1,0:T(4,128)S(1)}, u32[]{:S(2)}, u32[]{:S(2)}) collective-permute-start(f32[4,128]{1,0:T(4,128)S(1)} %slice.7), channel_id=1, source_target_pairs={{0,160},{32,128},{64,224},{96,192},{128,32},{160,0},{192,96},{224,... | collective-permute-start | bytes 6152 | tf_op jit(solution)/shard_map/ppermute | solution.py:400
  32.6 4.2 %collective-permute-start.10 = (f32[4,128]{1,0:T(4,128)S(1)}, f32[4,128]{1,0:T(4,128)S(1)}, u32[]{:S(2)}, u32[]{:S(2)}) collective-permute-start(f32[4,128]{1,0:T(4,128)S(1)} %slice.7), channel_id=1, source_target_pairs={{0,224},{32,192},{64,160},{96,128},{128,96},{160,64},{192,32},{224... | collective-permute-start | bytes 6152 | tf_op jit(solution)/shard_map/ppermute | solution.py:400
  33.7 3.1 %collective-permute-start.11 = (f32[4,128]{1,0:T(4,128)S(1)}, f32[4,128]{1,0:T(4,128)S(1)}, u32[]{:S(2)}, u32[]{:S(2)}) collective-permute-start(f32[4,128]{1,0:T(4,128)S(1)} %slice.7), channel_id=1, source_target_pairs={{0,96},{32,64},{64,32},{96,0},{128,224},{160,192},{192,160},{224,1... | collective-permute-start | bytes 6152 | tf_op jit(solution)/shard_map/ppermute | solution.py:400

commit v3 on v2

--- a/solution.py
+++ b/solution.py
@@ -22,8 +22,6 @@
 BF16 = jnp.bfloat16
 HIGH = lax.Precision.HIGHEST
 VMEM = pl.BlockSpec(memory_space=pltpu.VMEM)
-SMEM = pl.BlockSpec(memory_space=pltpu.SMEM)
-ANY = pl.BlockSpec(memory_space=pl.ANY)
 FIRST_LIMIT = 40 * 2**20
 PARAMS = pltpu.CompilerParams(vmem_limit_bytes=40 * 1024 * 1024)
 NN = (((1,), (0,)), ((), ()))
@@ -231,15 +229,16 @@
     start = (LEVELS - 1) * SW
     vm_row = scale_ref[LEVELS : LEVELS + 1, :]
     acc = jnp.zeros((8, ELEMS), F32)
-    totals = []
+    turned = [jnp.zeros((8, 128), F32) for _ in range(VERTS // 128)]
     for g in range(VERTS // 8):
         rows = slice(g * 8, g * 8 + 8)
         total = base_ref[rows, :]
         for t in range(TILES):
             at = start + t * 128
             total = total + q_ref[rows, at : at + 128] * alpha[t : t + 1, :]
-        totals.append(total)
         value = jnp.sum(total, axis=1, keepdims=True)
+        lane = iota((8, 128), 0) + (g % 16) * 8
+        turned[g // 16] = turned[g // 16] + jnp.where(iota((8, 128), 1) == lane, value, 0.0)
         vertex = (iota((8, ELEMS), 0) + g * 8).astype(F32)
         acc = acc + jnp.where(vertex == vm_row, value, 0.0)
     per_element = jnp.sum(acc, axis=0, keepdims=True)
@@ -250,9 +249,8 @@
         add = jnp.broadcast_to(rows[a * EY : (a + 1) * EY, None, :], (EY, NP, NZ)).reshape(NY, NZ)
         for i in range(NP):
             out_ref[a * NP + i] = local_ref[a * NP + i] + add
-    ones = jnp.ones((8, 128), BF16)
-    row = [bdot(ones, part.astype(BF16), NT) for part in split3(jnp.concatenate(totals, axis=0))]
-    sol_ref[...] = (row[0] + (row[1] + row[2]))[0:1]
+    for k, rows in enumerate(turned):
+        sol_ref[:, k * 128 : (k + 1) * 128] = jnp.sum(rows, axis=0, keepdims=True)
 
 
 LZ = EZ * PTS
@@ -260,7 +258,8 @@
 
 
 def prep_kernel(
-    lam_ref, vec_ref, scale_ref, bz0_ref, bz1_ref, in0_ref, in1_ref, f0_ref, f1_ref, k0_ref, k1_ref, inv_ref
+    lam_ref, vec_ref, scale_ref, r_ref, za_ref, zb_ref,
+    bz0_ref, bz1_ref, in0_ref, in1_ref, f0_ref, f1_ref, k0_ref, k1_ref, inv_ref, s0_ref, s1_ref,
 ):
     lane = iota((NZ + 8, LZ), 1)
     z = iota((NZ + 8, LZ), 0)
@@ -274,8 +273,20 @@
     for k in range(PTS):
         bz = jnp.where(place == k, v2[k : k + 1, :], bz)
     bz_in = jnp.where((place >= 1) & (place <= NP), bz, 0.0)[0:NZ]
-    bz0_ref[...], bz1_ref[...] = split(bz)
+    bz = split(bz)
+    bz0_ref[...], bz1_ref[...] = bz
     in0_ref[...], in1_ref[...] = split(bz_in)
+
+    row = iota((8, 128), 0)
+    side = odd("gz")
+    za, zb = za_ref[0:4, :], inside("gz", zb_ref[...])
+    zlow, zhigh = jnp.where(side == 1, za, zb), jnp.where(side == 1, zb, za)
+    sides = [
+        jnp.where(row == 0, zlow[k : k + 1], jnp.where(row == 1, zhigh[k : k + 1], 0.0)).T
+        for k in range(4)
+    ]
+    own = jnp.concatenate([r_ref[...].reshape(NX * NY, NZ), jnp.concatenate(sides, axis=0)], axis=1)
+    s0_ref[...], s1_ref[...] = split(dot3(split(own), bz))
 
     _, n = div_mod(iota((PTS, LXY), 1), PTS)
     m, _ = div_mod(iota((PTS, LXY), 1), PTS * EY)
@@ -316,37 +327,23 @@
 
 
 def local_kernel(
-    other, r_ref, za_ref, zb_ref, face_ref,
-    bz0_ref, bz1_ref, f0_ref, f1_ref, k0_ref, k1_ref, inv_ref, out_ref,
+    other, s0_ref, s1_ref, face_ref,
+    bz0_ref, bz1_ref, f0_ref, f1_ref, k0_ref, k1_ref, inv_ref, out_ref, w0_ref, w1_ref,
 ):
-    row = iota((8, 128), 0)
-    side = odd("gz")
-    za, zb = za_ref[0:4, :], inside("gz", zb_ref[...])
-    zlow, zhigh = jnp.where(side == 1, za, zb), jnp.where(side == 1, zb, za)
     face = face_ref[0:FACE, :]
     if other:
         face = inside("xy", face)
     at = odd("xy") if other else 1 - odd("xy")
-    before = at == 0
-    sides = [
-        jnp.where(row == 0, zlow[k : k + 1], jnp.where(row == 1, zhigh[k : k + 1], 0.0)).T
-        for k in range(4)
-    ]
-    edge = face[NY:FACE].T[0:NY]
-    own = r_ref[pl.ds(at * (NP - 1), NP + 1)].reshape((NP + 1) * NY, NZ)
-    sides = jnp.concatenate(sides, axis=0)
-    sides = jnp.where(before, sides[: (NP + 1) * NY], sides[(NP - 1) * NY :])
-    points = jnp.where(
-        before,
-        jnp.concatenate([face[0:NY], own], axis=0),
-        jnp.concatenate([own, face[0:NY]], axis=0),
-    )
-    sides = jnp.where(
-        before, jnp.concatenate([edge, sides], axis=0), jnp.concatenate([sides, edge], axis=0)
-    )
-    points = jnp.concatenate([points, sides], axis=1)
-    window = split(dot3(split(points), (bz0_ref[...], bz1_ref[...])))
-    scaled = dot3((f0_ref[...], f1_ref[...]), window) * inv_ref[at]
+    points = jnp.concatenate([face[0:NY], face[NY:FACE].T[0:NY]], axis=1)
+    edge = split(dot3(split(points), (bz0_ref[...], bz1_ref[...])))
+    size = (NP + 1) * NY
+    own_from = pl.multiple_of(at * ((NP - 1) * NY), NY)
+    own_to = pl.multiple_of((1 - at) * NY, NY)
+    edge_to = pl.multiple_of(at * size, NY)
+    for s_ref, w_ref, part in ((s0_ref, w0_ref, edge[0]), (s1_ref, w1_ref, edge[1])):
+        w_ref[pl.ds(own_to, size), :] = s_ref[pl.ds(own_from, size), :]
+        w_ref[pl.ds(edge_to, NY), :] = part
+    scaled = dot3((f0_ref[...], f1_ref[...]), (w0_ref[...], w1_ref[...])) * inv_ref[at]
     out_ref[...] = dot3((k0_ref[...], k1_ref[...]), split(scaled))
 
 
@@ -447,24 +444,26 @@
         + (half(NZ, LZ),) * 2
         + (half(LXY, PTS * NY),) * 2
         + (half(NP * NY, LXY),) * 2
-        + (shape(EX, LXY, LZ),),
-        in_specs=[VMEM] * 3,
-        out_specs=(VMEM,) * 9,
+        + (shape(EX, LXY, LZ),)
+        + (half(NX * NY, LZ),) * 2,
+        in_specs=[VMEM] * 6,
+        out_specs=(VMEM,) * 11,
         compiler_params=PARAMS,
         cost_estimate=cost(1_000_000_000, 1_000_000),
         name="prep",
-    )(values, vectors, scale)
+    )(values, vectors, scale, points, z_a, z_b)
 
     def local(other, face):
         return pl.pallas_call(
             functools.partial(local_kernel, other),
             out_shape=shape(NP * NY, LZ),
-            in_specs=[VMEM] * 11,
+            in_specs=[VMEM] * 10,
             out_specs=VMEM,
+            scratch_shapes=[pltpu.VMEM((PTS * NY, LZ), BF16)] * 2,
             compiler_params=PARAMS,
             cost_estimate=cost(1_000_000_000, 1_000_000),
             name="local",
-        )(points, z_a, z_b, face, *matrices[:2], *matrices[4:])
+        )(*matrices[9:], face, *matrices[:2], *matrices[4:9])
 
     total, matrices, message_b = lax.optimization_barrier((total, matrices, message_b))
     x_b = pairs(message_b, "xy")

time: 38 us -> 37.6 us (0.989)
    pallas_call x2, Pallas kernels: 3.41 us -> 2.81 us  [local(): pl.pallas_call(functools.partial(local_kernel, other), out_shape=shape(NP...]
  transfers between devices with their start and end apart: 13 -> 13, of which waited for: 5 -> 5; matrix products, arithmetic and copies ran while one was open for 0% -> 0% of each run, Pallas kernels for 15% -> 14%
where the time goes in v3:
time: 37.6 us
  starting transfers between devices  21.9 us (58%)
  Pallas kernels  9.51 us (25%)
  waiting for transfers between devices  5.09 us (14%)
  between operations  0.74 us (2%)
    ppermute x6, starting transfers between devices, cross(): lax.ppermute(value, ('gz', 'xy'), [(i, i ^ partner) for i in range(count)])  13.4 us
    ppermute x5, starting transfers between devices, swap(): lax.ppermute(value, axis, [(i, i ^ bits) for i in range(lax.axis_size(axi...  6.58 us
    pallas_call x1, Pallas kernels, per_device(): pl.pallas_call(first_kernel, out_shape=(shape(8 + PARTIALS, 128), shape(4...  3.17 us
    pallas_call x2, Pallas kernels, local(): pl.pallas_call(functools.partial(local_kernel, other), out_shape=shape(NP...  2.81 us
    ppermute x5, waiting for transfers between devices, swap(): lax.ppermute(value, axis, [(i, i ^ bits) for i in range(lax.axis_size(axi...  2.65 us
    ppermute x6, waiting for transfers between devices, cross(): lax.ppermute(value, ('gz', 'xy'), [(i, i ^ partner) for i in range(count)])  2.44 us
    ppermute x2, starting transfers between devices, pairs(): lax.ppermute(value, axis, [(i, (i + 2 * (i % 2) - 1) % count) for i in ra...  1.94 us
    pallas_call x1, Pallas kernels, per_device(): pl.pallas_call(prep_kernel, out_shape=(half(NZ + 8, LZ),) * 2 + (half(NZ,...  1.37 us
  transfers between devices with their start and end apart: 13, of which 5 were waited for; matrix products, arithmetic and copies ran while one was open for 0% of the time, Pallas kernels for 14%

profile of v3, /device:TPU:1, one launch (start us, length us, event | category | flops | bytes accessed | tf_op | source)
XLA Modules:
  0.0 37.6 jit_solution(14098200422888422146)
XLA Ops:
  0.6 3.2 %first.1 = (f32[32,128]{1,0:T(8,128)S(1)}, f32[4,128]{1,0:T(4,128)S(1)}, f32[24,128]{1,0:T(8,128)S(1)}, f32[8,128]{1,0:T(8,128)S(1)}, f32[16,32,128]{2,1,0:T(8,1...) custom-call(f32[16,32,128]{2,1,0:T(8,128)} %r_hbm.1, ...), custom_call_target="tpu_custom_call" | custom-call | flops 3145728 | bytes 6500000 | tf_op jit(solution)/shard_map/first/pallas_call | solution.py:368
  3.8 0.0 copy-start
  3.8 3.3 %collective-permute-start = (f32[32,128]{1,0:T(8,128)S(1)}, f32[32,128]{1,0:T(8,128)S(1)}, u32[]{:S(2)}, u32[]{:S(2)}) collective-permute-start(f32[32,128]{1,0:T(8,128)S(1)} %get-tuple-element.47), channel_id=1, source_target_pairs={{0,32},{32,0},{64,96},{96,64},{128,160},{160,128},{192,224},{224,1... | collective-permute-start | bytes 49160 | tf_op jit(solution)/shard_map/ppermute | solution.py:397
  7.2 0.0 collective-permute-start.1
  7.2 0.8 %collective-permute-done.za_ref = f32[32,128]{1,0:T(8,128)S(1)} collective-permute-done((f32[32,128]{1,0:T(8,128)S(1)}, f32[32,128]{1,0:T(8,128)S(1)}, u32[]{:S(2)}, u32[]{:S(2)}) %collective-permute-start) | collective-permute-done | bytes 16416 | tf_op jit(solution)/shard_map/ppermute | solution.py:397
  8.0 3.4 %collective-permute-start.3 = (f32[44,128]{1,0:T(8,128)S(1)}, f32[44,128]{1,0:T(8,128)S(1)}, u32[]{:S(2)}, u32[]{:S(2)}) collective-permute-start(f32[44,128]{1,0:T(8,128)S(1)} %join.1.sums_ref), channel_id=1, source_target_pairs={{0,34},{1,35},{2,32},{3,33},{4,38},{5,39},{6,36},{7,37},{8,42},{9,... | collective-permute-start | bytes 67592 | tf_op jit(solution)/shard_map/ppermute | solution.py:435
  11.4 1.5 %collective-permute-start.4 = (f32[44,128]{1,0:T(8,128)S(1)}, f32[44,128]{1,0:T(8,128)S(1)}, u32[]{:S(2)}, u32[]{:S(2)}) collective-permute-start(f32[44,128]{1,0:T(8,128)S(1)} %join.1.sums_ref), channel_id=1, source_target_pairs={{0,35},{1,34},{2,33},{3,32},{4,39},{5,38},{6,37},{7,36},{8,43},{9,... | collective-permute-start | bytes 67592 | tf_op jit(solution)/shard_map/ppermute | solution.py:435
  12.8 0.0 collective-permute-done.1.zb_ref
  12.8 0.1 edges.1
  13.0 0.2 collective-permute-start.2
  13.1 1.4 %prep.1 = (bf16[136,160]{1,0:T(8,128)(2,1)S(1)}, bf16[136,160]{1,0:T(8,128)(2,1)S(1)}, bf16[128,160]{1,0:T(8,128)(2,1)S(1)}, bf16[128,160]{1,0:T(8,128)(2,1)S(1)...) custom-call(f32[3,10]{1,0:T(4,128)S(1)} %get-tuple-element.51.lam_re, ...), custom_call_target="tpu_custom_call" | custom-call | flops 1000000000 | bytes 1000000 | tf_op jit(solution)/shard_map/prep/pallas_call | solution.py:441
  14.5 0.0 collective-permute-done.3
  14.5 2.0 %collective-permute-done.4 = f32[44,128]{1,0:T(8,128)S(1)} collective-permute-done((f32[44,128]{1,0:T(8,128)S(1)}, f32[44,128]{1,0:T(8,128)S(1)}, u32[]{:S(2)}, u32[]{:S(2)}) %collective-permute-start.4) | collective-permute-done | bytes 22560 | tf_op jit(solution)/shard_map/ppermute | solution.py:435
  16.5 0.0 collective-permute-done.2.face_ref
  16.5 0.1 fusion
  16.6 4.3 %collective-permute-start.5 = (f32[44,128]{1,0:T(8,128)S(1)}, f32[44,128]{1,0:T(8,128)S(1)}, u32[]{:S(2)}, u32[]{:S(2)}) collective-permute-start(f32[44,128]{1,0:T(8,128)S(1)} %fusion), channel_id=1, source_target_pairs={{0,38},{1,39},{2,36},{3,37},{4,34},{5,35},{6,32},{7,33},{8,46},{9,... | collective-permute-start | bytes 67592 | tf_op jit(solution)/shard_map/ppermute | solution.py:435
  20.9 1.9 %collective-permute-start.9 = (f32[40,128]{1,0:T(8,128)S(1)}, f32[40,128]{1,0:T(8,128)S(1)}, u32[]{:S(2)}, u32[]{:S(2)}) collective-permute-start(f32[40,128]{1,0:T(8,128)S(1)} %get-tuple-element.77), channel_id=1, source_target_pairs={{0,31},{1,2},{2,1},{3,4},{4,3},{5,6},{6,5},{7,8},{8,7},{9,10},{10,... | collective-permute-start | bytes 61448 | tf_op jit(solution)/shard_map/ppermute | solution.py:401
  22.8 1.4 %local.2.near_ref = f32[256,160]{1,0:T(8,128)S(1)} custom-call(bf16[512,160]{1,0:T(8,128)(2,1)S(1)} %get-tuple-element.67.s0_ref, bf16[512,160]{1,0:T(8,128)(2,1)S(1)} %get-tuple-element.68.s1_ref, f32[84,128]{1,0:T(8,128)S(1)} %collective-permute-done.2.face_ref, bf16[136,160]{1,0:T(8,128)(2,1)S(1)} %get-tuple-element.69.bz0_ref, ...), custom_call_target="tpu_custom_call" | custom-call | flops 1000000000 | bytes 1000000 | tf_op jit(solution)/shard_map/local/pallas_call | solution.py:457
  24.2 0.0 collective-permute-done.5
  24.2 0.1 select_add_fusion.1
  24.3 1.7 %collective-permute-start.7 = (f32[44,128]{1,0:T(8,128)S(1)}, f32[44,128]{1,0:T(8,128)S(1)}, u32[]{:S(2)}, u32[]{:S(2)}) collective-permute-start(f32[44,128]{1,0:T(8,128)S(1)} %select_add_fusion.1), channel_id=1, source_target_pairs={{0,48},{1,49},{2,50},{3,51},{4,52},{5,53},{6,54},{7,55},{8,56},{9,... | collective-permute-start | bytes 67592 | tf_op jit(solution)/shard_map/ppermute | solution.py:435
  26.0 0.4 %collective-permute-start.8 = (f32[44,128]{1,0:T(8,128)S(1)}, f32[44,128]{1,0:T(8,128)S(1)}, u32[]{:S(2)}, u32[]{:S(2)}) collective-permute-start(f32[44,128]{1,0:T(8,128)S(1)} %select_add_fusion.1), channel_id=1, source_target_pairs={{0,56},{1,57},{2,58},{3,59},{4,60},{5,61},{6,62},{7,63},{8,48},{9,... | collective-permute-start | bytes 67592 | tf_op jit(solution)/shard_map/ppermute | solution.py:435
  26.5 2.1 %collective-permute-start.6 = (f32[44,128]{1,0:T(8,128)S(1)}, f32[44,128]{1,0:T(8,128)S(1)}, u32[]{:S(2)}, u32[]{:S(2)}) collective-permute-start(f32[44,128]{1,0:T(8,128)S(1)} %select_add_fusion.1), channel_id=1, source_target_pairs={{0,40},{1,41},{2,42},{3,43},{4,44},{5,45},{6,46},{7,47},{8,32},{9,... | collective-permute-start | bytes 67592 | tf_op jit(solution)/shard_map/ppermute | solution.py:435
  28.6 0.0 collective-permute-done.9.face_ref
  28.6 1.4 %local.3.far_ref = f32[256,160]{1,0:T(8,128)S(1)} custom-call(bf16[512,160]{1,0:T(8,128)(2,1)S(1)} %get-tuple-element.67.s0_ref, bf16[512,160]{1,0:T(8,128)(2,1)S(1)} %get-tuple-element.68.s1_ref, f32[40,128]{1,0:T(8,128)S(1)} %collective-permute-done.9.face_ref, bf16[136,160]{1,0:T(8,128)(2,1)S(1)} %get-tuple-element.69.bz0_ref, ...), custom_call_target="tpu_custom_call" | custom-call | flops 1000000000 | bytes 1000000 | tf_op jit(solution)/shard_map/local/pallas_call | solution.py:457
  30.0 0.0 collective-permute-done.7
  30.0 0.5 %collective-permute-done.8 = f32[44,128]{1,0:T(8,128)S(1)} collective-permute-done((f32[44,128]{1,0:T(8,128)S(1)}, f32[44,128]{1,0:T(8,128)S(1)}, u32[]{:S(2)}, u32[]{:S(2)}) %collective-permute-start.8) | collective-permute-done | bytes 22560 | tf_op jit(solution)/shard_map/ppermute | solution.py:435
  30.5 0.0 collective-permute-done.6
  30.5 0.1 select_add_fusion.alpha_ref
  30.6 1.7 %collective-permute-start.12 = (f32[4,128]{1,0:T(4,128)S(1)}, f32[4,128]{1,0:T(4,128)S(1)}, u32[]{:S(2)}, u32[]{:S(2)}) collective-permute-start(f32[4,128]{1,0:T(4,128)S(1)} %slice.7), channel_id=1, source_target_pairs={{0,160},{32,128},{64,224},{96,192},{128,32},{160,0},{192,96},{224,... | collective-permute-start | bytes 6152 | tf_op jit(solution)/shard_map/ppermute | solution.py:397
  32.3 1.1 %collective-permute-start.10 = (f32[4,128]{1,0:T(4,128)S(1)}, f32[4,128]{1,0:T(4,128)S(1)}, u32[]{:S(2)}, u32[]{:S(2)}) collective-permute-start(f32[4,128]{1,0:T(4,128)S(1)} %slice.7), channel_id=1, source_target_pairs={{0,224},{32,192},{64,160},{96,128},{128,96},{160,64},{192,32},{224... | collective-permute-start | bytes 6152 | tf_op jit(solution)/shard_map/ppermute | solution.py:397
  33.4 0.2 collective-permute-start.11
  33.7 0.0 copy-done
  33.7 1.0 %middle.1 = (f32[512,128]{1,0:T(8,128)S(1)}, f32[16,32,128]{2,1,0:T(8,128)S(1)}) custom-call(f32[8,128]{1,0:T(8,128)S(1)} %get-tuple-element.45.scale_ref, f32[44,128]{1,0:T(8,128)S(1)} %select_add_fusion.alpha_ref, f32[512,512]{1,0:T(8,128)S(1)} %copy-done, f32[512,3072]{1,0:T(8,128)S(1)} %get-tuple-element.79.q_ref, f32[256,160]{1,0:T(8,128)S(1)} %local.2.near_ref, ...), custom_call_target="tpu_custom_call" | custom-call | flops 3670016 | bytes 7000000 | tf_op jit(solution)/shard_map/middle/pallas_call | solution.py:480
  34.7 0.5 %collective-permute-done.12 = f32[4,128]{1,0:T(4,128)S(1)} collective-permute-done((f32[4,128]{1,0:T(4,128)S(1)}, f32[4,128]{1,0:T(4,128)S(1)}, u32[]{:S(2)}, u32[]{:S(2)}) %collective-permute-start.12) | collective-permute-done | bytes 2080 | tf_op jit(solution)/shard_map/ppermute | solution.py:397
  35.2 1.3 %collective-permute-done.10 = f32[4,128]{1,0:T(4,128)S(1)} collective-permute-done((f32[4,128]{1,0:T(4,128)S(1)}, f32[4,128]{1,0:T(4,128)S(1)}, u32[]{:S(2)}, u32[]{:S(2)}) %collective-permute-start.10) | collective-permute-done | bytes 2080 | tf_op jit(solution)/shard_map/ppermute | solution.py:397
  36.5 0.0 collective-permute-done.11
  36.5 1.0 %final.1 = (f32[16,32,128]{2,1,0:T(8,128)}, f32[1,512]{1,0:T(1,128)}) custom-call(f32[8,128]{1,0:T(8,128)S(1)} %get-tuple-element.45.scale_ref, f32[4,128]{1,0:T(4,128)S(1)} %add_add_fusion.alpha_ref, f32[512,128]{1,0:T(8,128)S(1)} %get-tuple-element.84.base_ref, f32[16,32,128]{2,1,0:T(8,128)S(1)} %get-tuple-element.85.local_ref, ...), custom_call_target="tpu_custom_call" | custom-call | flops 524288 | bytes 1500000 | tf_op jit(solution)/shard_map/final/pallas_call | solution.py:490
  (6 shorter events, 0.1 us)
Async XLA Ops:
  3.8 29.9 %copy-start = (f32[512,512]{1,0:T(8,128)S(1)}, f32[512,512]{1,0:T(8,128)}, u32[]{:S(2)}) copy-start(f32[512,512]{1,0:T(8,128)} %leaf_ref.1) | copy-start | bytes 3145732
  3.8 4.2 %collective-permute-start = (f32[32,128]{1,0:T(8,128)S(1)}, f32[32,128]{1,0:T(8,128)S(1)}, u32[]{:S(2)}, u32[]{:S(2)}) collective-permute-start(f32[32,128]{1,0:T(8,128)S(1)} %get-tuple-element.47), channel_id=1, source_target_pairs={{0,32},{32,0},{64,96},{96,64},{128,160},{160,128},{192,224},{224,1... | collective-permute-start | bytes 49160 | tf_op jit(solution)/shard_map/ppermute | solution.py:397
  7.2 5.7 %collective-permute-start.1 = (f32[4,128]{1,0:T(4,128)S(1)}, f32[4,128]{1,0:T(4,128)S(1)}, u32[]{:S(2)}, u32[]{:S(2)}) collective-permute-start(f32[4,128]{1,0:T(4,128)S(1)} %get-tuple-element.49), channel_id=1, source_target_pairs={{0,224},{32,64},{64,32},{96,128},{128,96},{160,192},{192,160},{224... | collective-permute-start | bytes 6152 | tf_op jit(solution)/shard_map/ppermute | solution.py:401
  8.0 6.5 %collective-permute-start.3 = (f32[44,128]{1,0:T(8,128)S(1)}, f32[44,128]{1,0:T(8,128)S(1)}, u32[]{:S(2)}, u32[]{:S(2)}) collective-permute-start(f32[44,128]{1,0:T(8,128)S(1)} %join.1.sums_ref), channel_id=1, source_target_pairs={{0,34},{1,35},{2,32},{3,33},{4,38},{5,39},{6,36},{7,37},{8,42},{9,... | collective-permute-start | bytes 67592 | tf_op jit(solution)/shard_map/ppermute | solution.py:435
  11.4 5.2 %collective-permute-start.4 = (f32[44,128]{1,0:T(8,128)S(1)}, f32[44,128]{1,0:T(8,128)S(1)}, u32[]{:S(2)}, u32[]{:S(2)}) collective-permute-start(f32[44,128]{1,0:T(8,128)S(1)} %join.1.sums_ref), channel_id=1, source_target_pairs={{0,35},{1,34},{2,33},{3,32},{4,39},{5,38},{6,37},{7,36},{8,43},{9,... | collective-permute-start | bytes 67592 | tf_op jit(solution)/shard_map/ppermute | solution.py:435
  13.0 3.6 %collective-permute-start.2 = (f32[84,128]{1,0:T(8,128)S(1)}, f32[84,128]{1,0:T(8,128)S(1)}, u32[]{:S(2)}, u32[]{:S(2)}) collective-permute-start(f32[84,128]{1,0:T(8,128)S(1)} %get-tuple-element.50), channel_id=1, source_target_pairs={{0,1},{1,0},{2,3},{3,2},{4,5},{5,4},{6,7},{7,6},{8,9},{9,8},{10,11... | collective-permute-start | bytes 129032 | tf_op jit(solution)/shard_map/ppermute | solution.py:397
  16.6 7.6 %collective-permute-start.5 = (f32[44,128]{1,0:T(8,128)S(1)}, f32[44,128]{1,0:T(8,128)S(1)}, u32[]{:S(2)}, u32[]{:S(2)}) collective-permute-start(f32[44,128]{1,0:T(8,128)S(1)} %fusion), channel_id=1, source_target_pairs={{0,38},{1,39},{2,36},{3,37},{4,34},{5,35},{6,32},{7,33},{8,46},{9,... | collective-permute-start | bytes 67592 | tf_op jit(solution)/shard_map/ppermute | solution.py:435
  20.9 7.7 %collective-permute-start.9 = (f32[40,128]{1,0:T(8,128)S(1)}, f32[40,128]{1,0:T(8,128)S(1)}, u32[]{:S(2)}, u32[]{:S(2)}) collective-permute-start(f32[40,128]{1,0:T(8,128)S(1)} %get-tuple-element.77), channel_id=1, source_target_pairs={{0,31},{1,2},{2,1},{3,4},{4,3},{5,6},{6,5},{7,8},{8,7},{9,10},{10,... | collective-permute-start | bytes 61448 | tf_op jit(solution)/shard_map/ppermute | solution.py:401
  24.3 5.7 %collective-permute-start.7 = (f32[44,128]{1,0:T(8,128)S(1)}, f32[44,128]{1,0:T(8,128)S(1)}, u32[]{:S(2)}, u32[]{:S(2)}) collective-permute-start(f32[44,128]{1,0:T(8,128)S(1)} %select_add_fusion.1), channel_id=1, source_target_pairs={{0,48},{1,49},{2,50},{3,51},{4,52},{5,53},{6,54},{7,55},{8,56},{9,... | collective-permute-start | bytes 67592 | tf_op jit(solution)/shard_map/ppermute | solution.py:435
  26.0 4.5 %collective-permute-start.8 = (f32[44,128]{1,0:T(8,128)S(1)}, f32[44,128]{1,0:T(8,128)S(1)}, u32[]{:S(2)}, u32[]{:S(2)}) collective-permute-start(f32[44,128]{1,0:T(8,128)S(1)} %select_add_fusion.1), channel_id=1, source_target_pairs={{0,56},{1,57},{2,58},{3,59},{4,60},{5,61},{6,62},{7,63},{8,48},{9,... | collective-permute-start | bytes 67592 | tf_op jit(solution)/shard_map/ppermute | solution.py:435
  26.5 4.0 %collective-permute-start.6 = (f32[44,128]{1,0:T(8,128)S(1)}, f32[44,128]{1,0:T(8,128)S(1)}, u32[]{:S(2)}, u32[]{:S(2)}) collective-permute-start(f32[44,128]{1,0:T(8,128)S(1)} %select_add_fusion.1), channel_id=1, source_target_pairs={{0,40},{1,41},{2,42},{3,43},{4,44},{5,45},{6,46},{7,47},{8,32},{9,... | collective-permute-start | bytes 67592 | tf_op jit(solution)/shard_map/ppermute | solution.py:435
  30.6 4.6 %collective-permute-start.12 = (f32[4,128]{1,0:T(4,128)S(1)}, f32[4,128]{1,0:T(4,128)S(1)}, u32[]{:S(2)}, u32[]{:S(2)}) collective-permute-start(f32[4,128]{1,0:T(4,128)S(1)} %slice.7), channel_id=1, source_target_pairs={{0,160},{32,128},{64,224},{96,192},{128,32},{160,0},{192,96},{224,... | collective-permute-start | bytes 6152 | tf_op jit(solution)/shard_map/ppermute | solution.py:397
  32.3 4.2 %collective-permute-start.10 = (f32[4,128]{1,0:T(4,128)S(1)}, f32[4,128]{1,0:T(4,128)S(1)}, u32[]{:S(2)}, u32[]{:S(2)}) collective-permute-start(f32[4,128]{1,0:T(4,128)S(1)} %slice.7), channel_id=1, source_target_pairs={{0,224},{32,192},{64,160},{96,128},{128,96},{160,64},{192,32},{224... | collective-permute-start | bytes 6152 | tf_op jit(solution)/shard_map/ppermute | solution.py:397
  33.4 3.1 %collective-permute-start.11 = (f32[4,128]{1,0:T(4,128)S(1)}, f32[4,128]{1,0:T(4,128)S(1)}, u32[]{:S(2)}, u32[]{:S(2)}) collective-permute-start(f32[4,128]{1,0:T(4,128)S(1)} %slice.7), channel_id=1, source_target_pairs={{0,96},{32,64},{64,32},{96,0},{128,224},{160,192},{192,160},{224,1... | collective-permute-start | bytes 6152 | tf_op jit(solution)/shard_map/ppermute | solution.py:397

commit v4 on v3

--- a/solution.py
+++ b/solution.py
@@ -170,12 +170,22 @@
         copy.wait()
 
 
+def sums_row(level, core):
+    return TILES + (LEVELS - 2 - level) * 2 * TILES + core * TILES
+
+
+def sums_from(level):
+    return TILES + (LEVELS - 1 - level) * 2 * TILES
+
+
 def join_kernel(partial_ref, za_ref, out_ref):
     side = odd("gz") == 1
     mine, other = partial_ref[...], za_ref[8 : 8 + PARTIALS, :]
-    out_ref[0:LAST, :] = jnp.where(side, other, mine)[0:LAST]
-    out_ref[LAST : 2 * LAST, :] = jnp.where(side, mine, other)[0:LAST]
-    out_ref[2 * LAST : SUMS, :] = (mine + other)[LAST:]
+    out_ref[0:TILES, :] = (mine + other)[LAST:]
+    for core, rows in enumerate((jnp.where(side, other, mine), jnp.where(side, mine, other))):
+        for level in range(LEVELS - 1):
+            at = sums_row(level, core)
+            out_ref[at : at + TILES, :] = rows[level * TILES : (level + 1) * TILES]
 
 
 def edge_kernel(r_ref, za_ref, zb_ref, sums_ref, a_ref, b_ref):
@@ -212,7 +222,8 @@
     side = odd("gz") == 1
     for t in range((LEVELS - 1) * TILES):
         level = t // TILES
-        row = jnp.where(side, alpha_ref[LAST + t : LAST + t + 1, :], alpha_ref[t : t + 1, :])
+        even, odd_at = (sums_row(level, core) + t % TILES for core in range(2))
+        row = jnp.where(side, alpha_ref[odd_at : odd_at + 1, :], alpha_ref[even : even + 1, :])
         alpha.append(row * scale_ref[level : level + 1, :])
     for c in range(CHUNKS):
         rows = slice(c * ROWS, (c + 1) * ROWS)
@@ -423,20 +434,17 @@
         name="edges",
     )(points, z_a, z_b, total)
 
-    row = jnp.arange(SUMS, dtype=jnp.int32)[:, None]
-    level = jnp.where(row < 2 * LAST, row % LAST, LAST) // TILES
-
-    def from_level(value, first):
-        return jnp.where(level >= first, value, 0.0)
+    def widen(value):
+        return jnp.pad(value, ((0, SUMS - value.shape[0]), (0, 0)))
 
     def cross(value, bits):
         count = lax.axis_size("gz") * lax.axis_size("xy")
         partner = lax.axis_size("xy") ^ bits
         return lax.ppermute(value, ("gz", "xy"), [(i, i ^ partner) for i in range(count)])
 
-    two, three = cross(total, 2), cross(total, 3)
+    two, three = (cross(total[: sums_from(1)], bits) for bits in (3, 2))
     x_a = swap(message_a, "xy", 1)
-    total = total + x_a[FACE:] + from_level(two + three, 1)
+    total = total + x_a[FACE:] + widen(two + three)
     half = lambda *dims: jax.ShapeDtypeStruct(dims, BF16)
     matrices = pl.pallas_call(
         prep_kernel,
@@ -468,14 +476,15 @@
     total, matrices, message_b = lax.optimization_barrier((total, matrices, message_b))
     x_b = pairs(message_b, "xy")
     near = local(False, x_a)
-    total = total + from_level(cross(total, 6), 2)
+    total = total + widen(cross(total[: sums_from(2)], 6))
     total, near = lax.optimization_barrier((total, near))
     far = local(True, x_b)
-    one, two, three = (cross(total, bits) for bits in (8, 16, 24))
-    total = total + from_level(one, 3) + from_level(two + three, 4)
+    one = cross(total[: sums_from(3)], 8)
+    two, three = (cross(total[: sums_from(4)], bits) for bits in (24, 16))
+    total = total + widen(one) + widen(two + three)
     total, far = lax.optimization_barrier((total, far))
-    last = total[2 * LAST :]
-    last = last + (swap(last, "gz", 7) + swap(last, "gz", 3) + swap(last, "gz", 5))
+    last = total[:TILES]
+    last = last + (swap(last, "gz", 3) + swap(last, "gz", 7) + swap(last, "gz", 5))
 
     base, local = pl.pallas_call(
         middle_kernel,

time: 37.6 us -> 37.1 us (0.987)
  transfers between devices with their start and end apart: 13 -> 13, of which waited for: 5 -> 6; matrix products, arithmetic and copies ran while one was open for 0% -> 0% of each run, Pallas kernels for 14% -> 14%
where the time goes in v4:
time: 37.1 us
  starting transfers between devices  21.9 us (59%)
  Pallas kernels  9.51 us (26%)
  waiting for transfers between devices  4.89 us (13%)
  between operations  0.75 us (2%)
    ppermute x6, starting transfers between devices, cross(): lax.ppermute(value, ('gz', 'xy'), [(i, i ^ partner) for i in range(count)])  13.5 us
    ppermute x5, starting transfers between devices, swap(): lax.ppermute(value, axis, [(i, i ^ bits) for i in range(lax.axis_size(axi...  6.49 us
    pallas_call x1, Pallas kernels, per_device(): pl.pallas_call(first_kernel, out_shape=(shape(8 + PARTIALS, 128), shape(4...  3.17 us
    pallas_call x2, Pallas kernels, local(): pl.pallas_call(functools.partial(local_kernel, other), out_shape=shape(NP...  2.81 us
    ppermute x5, waiting for transfers between devices, swap(): lax.ppermute(value, axis, [(i, i ^ bits) for i in range(lax.axis_size(axi...  2.66 us
    ppermute x6, waiting for transfers between devices, cross(): lax.ppermute(value, ('gz', 'xy'), [(i, i ^ partner) for i in range(count)])  2.22 us
    ppermute x2, starting transfers between devices, pairs(): lax.ppermute(value, axis, [(i, (i + 2 * (i % 2) - 1) % count) for i in ra...  1.91 us
    pallas_call x1, Pallas kernels, per_device(): pl.pallas_call(prep_kernel, out_shape=(half(NZ + 8, LZ),) * 2 + (half(NZ,...  1.37 us
  transfers between devices with their start and end apart: 13, of which 6 were waited for; matrix products, arithmetic and copies ran while one was open for 0% of the time, Pallas kernels for 14%

profile of v4, /device:TPU:1, one launch (start us, length us, event | category | flops | bytes accessed | tf_op | source)
XLA Modules:
  0.0 37.1 jit_solution(3087786252995359190)
XLA Ops:
  0.6 3.2 %first.1 = (f32[32,128]{1,0:T(8,128)S(1)}, f32[4,128]{1,0:T(4,128)S(1)}, f32[24,128]{1,0:T(8,128)S(1)}, f32[8,128]{1,0:T(8,128)S(1)}, f32[16,32,128]{2,1,0:T(8,1...) custom-call(f32[16,32,128]{2,1,0:T(8,128)} %r_hbm.1, ...), custom_call_target="tpu_custom_call" | custom-call | flops 3145728 | bytes 6500000 | tf_op jit(solution)/shard_map/first/pallas_call | solution.py:379
  3.8 0.0 copy-start
  3.8 3.3 %collective-permute-start = (f32[32,128]{1,0:T(8,128)S(1)}, f32[32,128]{1,0:T(8,128)S(1)}, u32[]{:S(2)}, u32[]{:S(2)}) collective-permute-start(f32[32,128]{1,0:T(8,128)S(1)} %get-tuple-element.47), channel_id=1, source_target_pairs={{0,32},{32,0},{64,96},{96,64},{128,160},{160,128},{192,224},{224,1... | collective-permute-start | bytes 49160 | tf_op jit(solution)/shard_map/ppermute | solution.py:408
  7.2 0.0 collective-permute-start.1
  7.2 0.8 %collective-permute-done.za_ref = f32[32,128]{1,0:T(8,128)S(1)} collective-permute-done((f32[32,128]{1,0:T(8,128)S(1)}, f32[32,128]{1,0:T(8,128)S(1)}, u32[]{:S(2)}, u32[]{:S(2)}) %collective-permute-start) | collective-permute-done | bytes 16416 | tf_op jit(solution)/shard_map/ppermute | solution.py:408
  8.0 3.3 %collective-permute-start.4 = (f32[36,128]{1,0:T(8,128)S(1)}, f32[36,128]{1,0:T(8,128)S(1)}, u32[]{:S(2)}, u32[]{:S(2)}) collective-permute-start(f32[36,128]{1,0:T(8,128)S(1)} %slice.27), channel_id=1, source_target_pairs={{0,34},{1,35},{2,32},{3,33},{4,38},{5,39},{6,36},{7,37},{8,42},{9,... | collective-permute-start | bytes 55304 | tf_op jit(solution)/shard_map/ppermute | solution.py:443
  11.3 1.5 %collective-permute-start.3 = (f32[36,128]{1,0:T(8,128)S(1)}, f32[36,128]{1,0:T(8,128)S(1)}, u32[]{:S(2)}, u32[]{:S(2)}) collective-permute-start(f32[36,128]{1,0:T(8,128)S(1)} %slice.27), channel_id=1, source_target_pairs={{0,35},{1,34},{2,33},{3,32},{4,39},{5,38},{6,37},{7,36},{8,43},{9,... | collective-permute-start | bytes 55304 | tf_op jit(solution)/shard_map/ppermute | solution.py:443
  12.7 0.0 collective-permute-done.1.zb_ref
  12.7 0.1 edges.1
  12.9 0.2 collective-permute-start.2
  13.1 1.4 %prep.1 = (bf16[136,160]{1,0:T(8,128)(2,1)S(1)}, bf16[136,160]{1,0:T(8,128)(2,1)S(1)}, bf16[128,160]{1,0:T(8,128)(2,1)S(1)}, bf16[128,160]{1,0:T(8,128)(2,1)S(1)...) custom-call(f32[3,10]{1,0:T(4,128)S(1)} %get-tuple-element.51.lam_re, ...), custom_call_target="tpu_custom_call" | custom-call | flops 1000000000 | bytes 1000000 | tf_op jit(solution)/shard_map/prep/pallas_call | solution.py:449
  14.4 0.0 collective-permute-done.4
  14.5 1.9 %collective-permute-done.3 = f32[36,128]{1,0:T(8,128)S(1)} collective-permute-done((f32[36,128]{1,0:T(8,128)S(1)}, f32[36,128]{1,0:T(8,128)S(1)}, u32[]{:S(2)}, u32[]{:S(2)}) %collective-permute-start.3) | collective-permute-done | bytes 18464 | tf_op jit(solution)/shard_map/ppermute | solution.py:443
  16.4 0.0 collective-permute-done.2.face_ref
  16.4 4.4 %collective-permute-start.5 = (f32[28,128]{1,0:T(8,128)S(1)}, f32[28,128]{1,0:T(8,128)S(1)}, u32[]{:S(2)}, u32[]{:S(2)}) collective-permute-start(f32[28,128]{1,0:T(8,128)S(1)} %slice.22), channel_id=1, source_target_pairs={{0,38},{1,39},{2,36},{3,37},{4,34},{5,35},{6,32},{7,33},{8,46},{9,... | collective-permute-start | bytes 43016 | tf_op jit(solution)/shard_map/ppermute | solution.py:443
  20.8 1.9 %collective-permute-start.9 = (f32[40,128]{1,0:T(8,128)S(1)}, f32[40,128]{1,0:T(8,128)S(1)}, u32[]{:S(2)}, u32[]{:S(2)}) collective-permute-start(f32[40,128]{1,0:T(8,128)S(1)} %get-tuple-element.77), channel_id=1, source_target_pairs={{0,31},{1,2},{2,1},{3,4},{4,3},{5,6},{6,5},{7,8},{8,7},{9,10},{10,... | collective-permute-start | bytes 61448 | tf_op jit(solution)/shard_map/ppermute | solution.py:412
  22.7 1.4 %local.2.near_ref = f32[256,160]{1,0:T(8,128)S(1)} custom-call(bf16[512,160]{1,0:T(8,128)(2,1)S(1)} %get-tuple-element.67.s0_ref, bf16[512,160]{1,0:T(8,128)(2,1)S(1)} %get-tuple-element.68.s1_ref, f32[84,128]{1,0:T(8,128)S(1)} %collective-permute-done.2.face_ref, bf16[136,160]{1,0:T(8,128)(2,1)S(1)} %get-tuple-element.69.bz0_ref, ...), custom_call_target="tpu_custom_call" | custom-call | flops 1000000000 | bytes 1000000 | tf_op jit(solution)/shard_map/local/pallas_call | solution.py:465
  24.1 0.0 collective-permute-done.5
  24.2 1.8 %collective-permute-start.8 = (f32[12,128]{1,0:T(8,128)S(1)}, f32[12,128]{1,0:T(8,128)S(1)}, u32[]{:S(2)}, u32[]{:S(2)}) collective-permute-start(f32[12,128]{1,0:T(8,128)S(1)} %slice.24), channel_id=1, source_target_pairs={{0,48},{1,49},{2,50},{3,51},{4,52},{5,53},{6,54},{7,55},{8,56},{9,... | collective-permute-start | bytes 18440 | tf_op jit(solution)/shard_map/ppermute | solution.py:443
  26.0 0.3 collective-permute-start.7
  26.3 2.2 %collective-permute-start.6 = (f32[20,128]{1,0:T(8,128)S(1)}, f32[20,128]{1,0:T(8,128)S(1)}, u32[]{:S(2)}, u32[]{:S(2)}) collective-permute-start(f32[20,128]{1,0:T(8,128)S(1)} %slice.23), channel_id=1, source_target_pairs={{0,40},{1,41},{2,42},{3,43},{4,44},{5,45},{6,46},{7,47},{8,32},{9,... | collective-permute-start | bytes 30728 | tf_op jit(solution)/shard_map/ppermute | solution.py:443
  28.5 0.0 collective-permute-done.9.face_ref
  28.6 1.4 %local.3.far_ref = f32[256,160]{1,0:T(8,128)S(1)} custom-call(bf16[512,160]{1,0:T(8,128)(2,1)S(1)} %get-tuple-element.67.s0_ref, bf16[512,160]{1,0:T(8,128)(2,1)S(1)} %get-tuple-element.68.s1_ref, f32[40,128]{1,0:T(8,128)S(1)} %collective-permute-done.9.face_ref, bf16[136,160]{1,0:T(8,128)(2,1)S(1)} %get-tuple-element.69.bz0_ref, ...), custom_call_target="tpu_custom_call" | custom-call | flops 1000000000 | bytes 1000000 | tf_op jit(solution)/shard_map/local/pallas_call | solution.py:465
  30.0 0.0 collective-permute-done.8
  30.0 0.3 collective-permute-done.7
  30.3 0.0 collective-permute-done.6
  30.3 1.3 %collective-permute-start.12 = (f32[4,128]{1,0:T(4,128)S(1)}, f32[4,128]{1,0:T(4,128)S(1)}, u32[]{:S(2)}, u32[]{:S(2)}) collective-permute-start(f32[4,128]{1,0:T(4,128)S(1)} %slice.25), channel_id=1, source_target_pairs={{0,160},{32,128},{64,224},{96,192},{128,32},{160,0},{192,96},{224,... | collective-permute-start | bytes 6152 | tf_op jit(solution)/shard_map/ppermute | solution.py:408
  31.6 1.5 %collective-permute-start.11 = (f32[4,128]{1,0:T(4,128)S(1)}, f32[4,128]{1,0:T(4,128)S(1)}, u32[]{:S(2)}, u32[]{:S(2)}) collective-permute-start(f32[4,128]{1,0:T(4,128)S(1)} %slice.25), channel_id=1, source_target_pairs={{0,224},{32,192},{64,160},{96,128},{128,96},{160,64},{192,32},{224... | collective-permute-start | bytes 6152 | tf_op jit(solution)/shard_map/ppermute | solution.py:408
  33.0 0.2 collective-permute-start.10
  33.3 0.0 copy-done
  33.3 1.0 %middle.1 = (f32[512,128]{1,0:T(8,128)S(1)}, f32[16,32,128]{2,1,0:T(8,128)S(1)}) custom-call(f32[8,128]{1,0:T(8,128)S(1)} %get-tuple-element.45.scale_ref, f32[44,128]{1,0:T(8,128)S(1)} %pad_add_fusion.alpha_ref, f32[512,512]{1,0:T(8,128)S(1)} %copy-done, f32[512,3072]{1,0:T(8,128)S(1)} %get-tuple-element.79.q_ref, f32[256,160]{1,0:T(8,128)S(1)} %local.2.near_ref, ...), custom_call_target="tpu_custom_call" | custom-call | flops 3670016 | bytes 7000000 | tf_op jit(solution)/shard_map/middle/pallas_call | solution.py:489
  34.3 0.6 %collective-permute-done.12 = f32[4,128]{1,0:T(4,128)S(1)} collective-permute-done((f32[4,128]{1,0:T(4,128)S(1)}, f32[4,128]{1,0:T(4,128)S(1)}, u32[]{:S(2)}, u32[]{:S(2)}) %collective-permute-start.12) | collective-permute-done | bytes 2080 | tf_op jit(solution)/shard_map/ppermute | solution.py:408
  34.9 0.9 %collective-permute-done.11 = f32[4,128]{1,0:T(4,128)S(1)} collective-permute-done((f32[4,128]{1,0:T(4,128)S(1)}, f32[4,128]{1,0:T(4,128)S(1)}, u32[]{:S(2)}, u32[]{:S(2)}) %collective-permute-start.11) | collective-permute-done | bytes 2080 | tf_op jit(solution)/shard_map/ppermute | solution.py:408
  35.8 0.2 collective-permute-done.10
  36.1 1.0 %final.1 = (f32[16,32,128]{2,1,0:T(8,128)}, f32[1,512]{1,0:T(1,128)}) custom-call(f32[8,128]{1,0:T(8,128)S(1)} %get-tuple-element.45.scale_ref, f32[4,128]{1,0:T(4,128)S(1)} %add_add_fusion.alpha_ref, f32[512,128]{1,0:T(8,128)S(1)} %get-tuple-element.84.base_ref, f32[16,32,128]{2,1,0:T(8,128)S(1)} %get-tuple-element.85.local_ref, ...), custom_call_target="tpu_custom_call" | custom-call | flops 524288 | bytes 1500000 | tf_op jit(solution)/shard_map/final/pallas_call | solution.py:499
  (12 shorter events, 0.1 us)
Async XLA Ops:
  3.8 29.4 %copy-start = (f32[512,512]{1,0:T(8,128)S(1)}, f32[512,512]{1,0:T(8,128)}, u32[]{:S(2)}) copy-start(f32[512,512]{1,0:T(8,128)} %leaf_ref.1) | copy-start | bytes 3145732
  3.8 4.2 %collective-permute-start = (f32[32,128]{1,0:T(8,128)S(1)}, f32[32,128]{1,0:T(8,128)S(1)}, u32[]{:S(2)}, u32[]{:S(2)}) collective-permute-start(f32[32,128]{1,0:T(8,128)S(1)} %get-tuple-element.47), channel_id=1, source_target_pairs={{0,32},{32,0},{64,96},{96,64},{128,160},{160,128},{192,224},{224,1... | collective-permute-start | bytes 49160 | tf_op jit(solution)/shard_map/ppermute | solution.py:408
  7.2 5.6 %collective-permute-start.1 = (f32[4,128]{1,0:T(4,128)S(1)}, f32[4,128]{1,0:T(4,128)S(1)}, u32[]{:S(2)}, u32[]{:S(2)}) collective-permute-start(f32[4,128]{1,0:T(4,128)S(1)} %get-tuple-element.49), channel_id=1, source_target_pairs={{0,224},{32,64},{64,32},{96,128},{128,96},{160,192},{192,160},{224... | collective-permute-start | bytes 6152 | tf_op jit(solution)/shard_map/ppermute | solution.py:412
  8.0 6.4 %collective-permute-start.4 = (f32[36,128]{1,0:T(8,128)S(1)}, f32[36,128]{1,0:T(8,128)S(1)}, u32[]{:S(2)}, u32[]{:S(2)}) collective-permute-start(f32[36,128]{1,0:T(8,128)S(1)} %slice.27), channel_id=1, source_target_pairs={{0,34},{1,35},{2,32},{3,33},{4,38},{5,39},{6,36},{7,37},{8,42},{9,... | collective-permute-start | bytes 55304 | tf_op jit(solution)/shard_map/ppermute | solution.py:443
  11.3 5.1 %collective-permute-start.3 = (f32[36,128]{1,0:T(8,128)S(1)}, f32[36,128]{1,0:T(8,128)S(1)}, u32[]{:S(2)}, u32[]{:S(2)}) collective-permute-start(f32[36,128]{1,0:T(8,128)S(1)} %slice.27), channel_id=1, source_target_pairs={{0,35},{1,34},{2,33},{3,32},{4,39},{5,38},{6,37},{7,36},{8,43},{9,... | collective-permute-start | bytes 55304 | tf_op jit(solution)/shard_map/ppermute | solution.py:443
  12.9 3.6 %collective-permute-start.2 = (f32[84,128]{1,0:T(8,128)S(1)}, f32[84,128]{1,0:T(8,128)S(1)}, u32[]{:S(2)}, u32[]{:S(2)}) collective-permute-start(f32[84,128]{1,0:T(8,128)S(1)} %get-tuple-element.50), channel_id=1, source_target_pairs={{0,1},{1,0},{2,3},{3,2},{4,5},{5,4},{6,7},{7,6},{8,9},{9,8},{10,11... | collective-permute-start | bytes 129032 | tf_op jit(solution)/shard_map/ppermute | solution.py:408
  16.4 7.7 %collective-permute-start.5 = (f32[28,128]{1,0:T(8,128)S(1)}, f32[28,128]{1,0:T(8,128)S(1)}, u32[]{:S(2)}, u32[]{:S(2)}) collective-permute-start(f32[28,128]{1,0:T(8,128)S(1)} %slice.22), channel_id=1, source_target_pairs={{0,38},{1,39},{2,36},{3,37},{4,34},{5,35},{6,32},{7,33},{8,46},{9,... | collective-permute-start | bytes 43016 | tf_op jit(solution)/shard_map/ppermute | solution.py:443
  20.8 7.7 %collective-permute-start.9 = (f32[40,128]{1,0:T(8,128)S(1)}, f32[40,128]{1,0:T(8,128)S(1)}, u32[]{:S(2)}, u32[]{:S(2)}) collective-permute-start(f32[40,128]{1,0:T(8,128)S(1)} %get-tuple-element.77), channel_id=1, source_target_pairs={{0,31},{1,2},{2,1},{3,4},{4,3},{5,6},{6,5},{7,8},{8,7},{9,10},{10,... | collective-permute-start | bytes 61448 | tf_op jit(solution)/shard_map/ppermute | solution.py:412
  24.2 5.8 %collective-permute-start.8 = (f32[12,128]{1,0:T(8,128)S(1)}, f32[12,128]{1,0:T(8,128)S(1)}, u32[]{:S(2)}, u32[]{:S(2)}) collective-permute-start(f32[12,128]{1,0:T(8,128)S(1)} %slice.24), channel_id=1, source_target_pairs={{0,48},{1,49},{2,50},{3,51},{4,52},{5,53},{6,54},{7,55},{8,56},{9,... | collective-permute-start | bytes 18440 | tf_op jit(solution)/shard_map/ppermute | solution.py:443
  26.0 4.3 %collective-permute-start.7 = (f32[12,128]{1,0:T(8,128)S(1)}, f32[12,128]{1,0:T(8,128)S(1)}, u32[]{:S(2)}, u32[]{:S(2)}) collective-permute-start(f32[12,128]{1,0:T(8,128)S(1)} %slice.24), channel_id=1, source_target_pairs={{0,56},{1,57},{2,58},{3,59},{4,60},{5,61},{6,62},{7,63},{8,48},{9,... | collective-permute-start | bytes 18440 | tf_op jit(solution)/shard_map/ppermute | solution.py:443
  26.3 3.9 %collective-permute-start.6 = (f32[20,128]{1,0:T(8,128)S(1)}, f32[20,128]{1,0:T(8,128)S(1)}, u32[]{:S(2)}, u32[]{:S(2)}) collective-permute-start(f32[20,128]{1,0:T(8,128)S(1)} %slice.23), channel_id=1, source_target_pairs={{0,40},{1,41},{2,42},{3,43},{4,44},{5,45},{6,46},{7,47},{8,32},{9,... | collective-permute-start | bytes 30728 | tf_op jit(solution)/shard_map/ppermute | solution.py:443
  30.3 4.6 %collective-permute-start.12 = (f32[4,128]{1,0:T(4,128)S(1)}, f32[4,128]{1,0:T(4,128)S(1)}, u32[]{:S(2)}, u32[]{:S(2)}) collective-permute-start(f32[4,128]{1,0:T(4,128)S(1)} %slice.25), channel_id=1, source_target_pairs={{0,160},{32,128},{64,224},{96,192},{128,32},{160,0},{192,96},{224,... | collective-permute-start | bytes 6152 | tf_op jit(solution)/shard_map/ppermute | solution.py:408
  31.6 4.3 %collective-permute-start.11 = (f32[4,128]{1,0:T(4,128)S(1)}, f32[4,128]{1,0:T(4,128)S(1)}, u32[]{:S(2)}, u32[]{:S(2)}) collective-permute-start(f32[4,128]{1,0:T(4,128)S(1)} %slice.25), channel_id=1, source_target_pairs={{0,224},{32,192},{64,160},{96,128},{128,96},{160,64},{192,32},{224... | collective-permute-start | bytes 6152 | tf_op jit(solution)/shard_map/ppermute | solution.py:408
  33.0 3.0 %collective-permute-start.10 = (f32[4,128]{1,0:T(4,128)S(1)}, f32[4,128]{1,0:T(4,128)S(1)}, u32[]{:S(2)}, u32[]{:S(2)}) collective-permute-start(f32[4,128]{1,0:T(4,128)S(1)} %slice.25), channel_id=1, source_target_pairs={{0,96},{32,64},{64,32},{96,0},{128,224},{160,192},{192,160},{224,1... | collective-permute-start | bytes 6152 | tf_op jit(solution)/shard_map/ppermute | solution.py:408

commit v5 on v4

--- a/solution.py
+++ b/solution.py
@@ -102,7 +102,7 @@
 
 def first_kernel(
     r_hbm, vm_hbm, mask_hbm, q_hbm, vec_hbm, lam_hbm, scale_hbm,
-    face_a_ref, face_b_ref, out_ref, aux_ref, r_ref, q_ref, vec_ref, lam_ref, scale_ref,
+    face_a_ref, face_b_ref, aux_ref, r_ref, q_ref, vec_ref, lam_ref, scale_ref,
     v_ref, m_ref, b_ref, sem,
 ):
     moves = (
@@ -164,7 +164,6 @@
                 acc[t] = acc[t] + q_ref[at : at + 8, t * 128 : (t + 1) * 128] * b
     for t in range(PARTIALS):
         total = jnp.sum(acc[t], axis=0, keepdims=True) * scales[t // TILES]
-        out_ref[t : t + 1, :] = total
         face_a_ref[8 + t : 9 + t, :] = total
     for copy in small[3:]:
         copy.wait()
@@ -178,9 +177,9 @@
     return TILES + (LEVELS - 1 - level) * 2 * TILES
 
 
-def join_kernel(partial_ref, za_ref, out_ref):
+def join_kernel(face_a_ref, za_ref, out_ref):
     side = odd("gz") == 1
-    mine, other = partial_ref[...], za_ref[8 : 8 + PARTIALS, :]
+    mine, other = face_a_ref[8 : 8 + PARTIALS, :], za_ref[8 : 8 + PARTIALS, :]
     out_ref[0:TILES, :] = (mine + other)[LAST:]
     for core, rows in enumerate((jnp.where(side, other, mine), jnp.where(side, mine, other))):
         for level in range(LEVELS - 1):
@@ -376,15 +375,15 @@
     separator_columns,
     separator_mask,
 ):
-    face_a, face_b, partial, aux, points, separators, vectors, values, scale = pl.pallas_call(
+    face_a, face_b, aux, points, separators, vectors, values, scale = pl.pallas_call(
         first_kernel,
         out_shape=(
-            shape(8 + PARTIALS, 128), shape(4, 128), shape(PARTIALS, 128), shape(8, 128),
+            shape(8 + PARTIALS, 128), shape(4, 128), shape(8, 128),
             shape(NX, NY, NZ), shape(VERTS, LEVELS * SW),
             shape(PTS, 3, PTS), shape(3, PTS), shape(EX, EY, EZ),
         ),
         in_specs=[pl.BlockSpec(memory_space=pltpu.HBM)] * 7,
-        out_specs=(VMEM,) * 9,
+        out_specs=(VMEM,) * 8,
         scratch_shapes=[
             pltpu.VMEM((EX, EY, EZ), jnp.int32),
             pltpu.VMEM((1, LEVELS), jnp.int32),
@@ -422,7 +421,7 @@
         compiler_params=PARAMS,
         cost_estimate=cost(1000, 50_000),
         name="join",
-    )(partial, z_a)
+    )(face_a, z_a)
 
     message_a, message_b = pl.pallas_call(
         edge_kernel,

time: 37.1 us -> 37.1 us (level)
  no operation moved by 1% of the time
where the time goes in v5:
time: 37.1 us
  starting transfers between devices  21.9 us (59%)
  Pallas kernels  9.51 us (26%)
  waiting for transfers between devices  4.89 us (13%)
  between operations  0.75 us (2%)
    ppermute x6, starting transfers between devices, cross(): lax.ppermute(value, ('gz', 'xy'), [(i, i ^ partner) for i in range(count)])  13.5 us
    ppermute x5, starting transfers between devices, swap(): lax.ppermute(value, axis, [(i, i ^ bits) for i in range(lax.axis_size(axi...  6.49 us
    pallas_call x1, Pallas kernels, per_device(): pl.pallas_call(first_kernel, out_shape=(shape(8 + PARTIALS, 128), shape(4...  3.17 us
    pallas_call x2, Pallas kernels, local(): pl.pallas_call(functools.partial(local_kernel, other), out_shape=shape(NP...  2.81 us
    ppermute x5, waiting for transfers between devices, swap(): lax.ppermute(value, axis, [(i, i ^ bits) for i in range(lax.axis_size(axi...  2.67 us
    ppermute x6, waiting for transfers between devices, cross(): lax.ppermute(value, ('gz', 'xy'), [(i, i ^ partner) for i in range(count)])  2.22 us
    ppermute x2, starting transfers between devices, pairs(): lax.ppermute(value, axis, [(i, (i + 2 * (i % 2) - 1) % count) for i in ra...  1.91 us
    pallas_call x1, Pallas kernels, per_device(): pl.pallas_call(prep_kernel, out_shape=(half(NZ + 8, LZ),) * 2 + (half(NZ,...  1.37 us
  transfers between devices with their start and end apart: 13, of which 6 were waited for; matrix products, arithmetic and copies ran while one was open for 0% of the time, Pallas kernels for 14%

profile of v5, /device:TPU:1, one launch (start us, length us, event | category | flops | bytes accessed | tf_op | source)
XLA Modules:
  0.0 37.1 jit_solution(6689538102683117613)
XLA Ops:
  0.6 3.2 %first.1 = (f32[32,128]{1,0:T(8,128)S(1)}, f32[4,128]{1,0:T(4,128)S(1)}, f32[8,128]{1,0:T(8,128)S(1)}, f32[16,32,128]{2,1,0:T(8,128)S(1)}, f32[512,3072]{1,0:T(8...) custom-call(f32[16,32,128]{2,1,0:T(8,128)} %r_hbm.1, s32[2,4,16]{2,1,0:T(4,128)} %vm_hbm.1, ...), custom_call_target="tpu_custom_call" | custom-call | flops 3145728 | bytes 6500000 | tf_op jit(solution)/shard_map/first/pallas_call | solution.py:378
  3.8 0.0 copy-start
  3.8 3.3 %collective-permute-start = (f32[32,128]{1,0:T(8,128)S(1)}, f32[32,128]{1,0:T(8,128)S(1)}, u32[]{:S(2)}, u32[]{:S(2)}) collective-permute-start(f32[32,128]{1,0:T(8,128)S(1)} %get-tuple-element.45.face_a_ref), channel_id=1, source_target_pairs={{0,32},{32,0},{64,96},{96,64},{128,160},{160,128},{192,224},{224,1... | collective-permute-start | bytes 49160 | tf_op jit(solution)/shard_map/ppermute | solution.py:407
  7.1 0.0 collective-permute-start.1
  7.2 0.8 %collective-permute-done.za_ref = f32[32,128]{1,0:T(8,128)S(1)} collective-permute-done((f32[32,128]{1,0:T(8,128)S(1)}, f32[32,128]{1,0:T(8,128)S(1)}, u32[]{:S(2)}, u32[]{:S(2)}) %collective-permute-start) | collective-permute-done | bytes 16416 | tf_op jit(solution)/shard_map/ppermute | solution.py:407
  8.0 3.3 %collective-permute-start.4 = (f32[36,128]{1,0:T(8,128)S(1)}, f32[36,128]{1,0:T(8,128)S(1)}, u32[]{:S(2)}, u32[]{:S(2)}) collective-permute-start(f32[36,128]{1,0:T(8,128)S(1)} %slice.27), channel_id=1, source_target_pairs={{0,34},{1,35},{2,32},{3,33},{4,38},{5,39},{6,36},{7,37},{8,42},{9,... | collective-permute-start | bytes 55304 | tf_op jit(solution)/shard_map/ppermute | solution.py:442
  11.3 1.5 %collective-permute-start.3 = (f32[36,128]{1,0:T(8,128)S(1)}, f32[36,128]{1,0:T(8,128)S(1)}, u32[]{:S(2)}, u32[]{:S(2)}) collective-permute-start(f32[36,128]{1,0:T(8,128)S(1)} %slice.27), channel_id=1, source_target_pairs={{0,35},{1,34},{2,33},{3,32},{4,39},{5,38},{6,37},{7,36},{8,43},{9,... | collective-permute-start | bytes 55304 | tf_op jit(solution)/shard_map/ppermute | solution.py:442
  12.7 0.0 collective-permute-done.1.zb_ref
  12.7 0.1 edges.1
  12.9 0.2 collective-permute-start.2
  13.1 1.4 %prep.1 = (bf16[136,160]{1,0:T(8,128)(2,1)S(1)}, bf16[136,160]{1,0:T(8,128)(2,1)S(1)}, bf16[128,160]{1,0:T(8,128)(2,1)S(1)}, bf16[128,160]{1,0:T(8,128)(2,1)S(1)...) custom-call(f32[3,10]{1,0:T(4,128)S(1)} %get-tuple-element.49.lam_re, ...), custom_call_target="tpu_custom_call" | custom-call | flops 1000000000 | bytes 1000000 | tf_op jit(solution)/shard_map/prep/pallas_call | solution.py:448
  14.4 0.0 collective-permute-done.4
  14.5 1.9 %collective-permute-done.3 = f32[36,128]{1,0:T(8,128)S(1)} collective-permute-done((f32[36,128]{1,0:T(8,128)S(1)}, f32[36,128]{1,0:T(8,128)S(1)}, u32[]{:S(2)}, u32[]{:S(2)}) %collective-permute-start.3) | collective-permute-done | bytes 18464 | tf_op jit(solution)/shard_map/ppermute | solution.py:442
  16.4 0.0 collective-permute-done.2.face_ref
  16.4 4.4 %collective-permute-start.5 = (f32[28,128]{1,0:T(8,128)S(1)}, f32[28,128]{1,0:T(8,128)S(1)}, u32[]{:S(2)}, u32[]{:S(2)}) collective-permute-start(f32[28,128]{1,0:T(8,128)S(1)} %slice.22), channel_id=1, source_target_pairs={{0,38},{1,39},{2,36},{3,37},{4,34},{5,35},{6,32},{7,33},{8,46},{9,... | collective-permute-start | bytes 43016 | tf_op jit(solution)/shard_map/ppermute | solution.py:442
  20.8 1.9 %collective-permute-start.9 = (f32[40,128]{1,0:T(8,128)S(1)}, f32[40,128]{1,0:T(8,128)S(1)}, u32[]{:S(2)}, u32[]{:S(2)}) collective-permute-start(f32[40,128]{1,0:T(8,128)S(1)} %get-tuple-element.75), channel_id=1, source_target_pairs={{0,31},{1,2},{2,1},{3,4},{4,3},{5,6},{6,5},{7,8},{8,7},{9,10},{10,... | collective-permute-start | bytes 61448 | tf_op jit(solution)/shard_map/ppermute | solution.py:411
  22.7 1.4 %local.2.near_ref = f32[256,160]{1,0:T(8,128)S(1)} custom-call(bf16[512,160]{1,0:T(8,128)(2,1)S(1)} %get-tuple-element.65.s0_ref, bf16[512,160]{1,0:T(8,128)(2,1)S(1)} %get-tuple-element.66.s1_ref, f32[84,128]{1,0:T(8,128)S(1)} %collective-permute-done.2.face_ref, bf16[136,160]{1,0:T(8,128)(2,1)S(1)} %get-tuple-element.67.bz0_ref, ...), custom_call_target="tpu_custom_call" | custom-call | flops 1000000000 | bytes 1000000 | tf_op jit(solution)/shard_map/local/pallas_call | solution.py:464
  24.1 0.0 collective-permute-done.5
  24.2 1.8 %collective-permute-start.8 = (f32[12,128]{1,0:T(8,128)S(1)}, f32[12,128]{1,0:T(8,128)S(1)}, u32[]{:S(2)}, u32[]{:S(2)}) collective-permute-start(f32[12,128]{1,0:T(8,128)S(1)} %slice.24), channel_id=1, source_target_pairs={{0,48},{1,49},{2,50},{3,51},{4,52},{5,53},{6,54},{7,55},{8,56},{9,... | collective-permute-start | bytes 18440 | tf_op jit(solution)/shard_map/ppermute | solution.py:442
  26.0 0.3 collective-permute-start.7
  26.3 2.2 %collective-permute-start.6 = (f32[20,128]{1,0:T(8,128)S(1)}, f32[20,128]{1,0:T(8,128)S(1)}, u32[]{:S(2)}, u32[]{:S(2)}) collective-permute-start(f32[20,128]{1,0:T(8,128)S(1)} %slice.23), channel_id=1, source_target_pairs={{0,40},{1,41},{2,42},{3,43},{4,44},{5,45},{6,46},{7,47},{8,32},{9,... | collective-permute-start | bytes 30728 | tf_op jit(solution)/shard_map/ppermute | solution.py:442
  28.5 0.0 collective-permute-done.9.face_ref
  28.5 1.4 %local.3.far_ref = f32[256,160]{1,0:T(8,128)S(1)} custom-call(bf16[512,160]{1,0:T(8,128)(2,1)S(1)} %get-tuple-element.65.s0_ref, bf16[512,160]{1,0:T(8,128)(2,1)S(1)} %get-tuple-element.66.s1_ref, f32[40,128]{1,0:T(8,128)S(1)} %collective-permute-done.9.face_ref, bf16[136,160]{1,0:T(8,128)(2,1)S(1)} %get-tuple-element.67.bz0_ref, ...), custom_call_target="tpu_custom_call" | custom-call | flops 1000000000 | bytes 1000000 | tf_op jit(solution)/shard_map/local/pallas_call | solution.py:464
  30.0 0.0 collective-permute-done.8
  30.0 0.3 collective-permute-done.7
  30.3 0.0 collective-permute-done.6
  30.3 1.3 %collective-permute-start.12 = (f32[4,128]{1,0:T(4,128)S(1)}, f32[4,128]{1,0:T(4,128)S(1)}, u32[]{:S(2)}, u32[]{:S(2)}) collective-permute-start(f32[4,128]{1,0:T(4,128)S(1)} %slice.25), channel_id=1, source_target_pairs={{0,160},{32,128},{64,224},{96,192},{128,32},{160,0},{192,96},{224,... | collective-permute-start | bytes 6152 | tf_op jit(solution)/shard_map/ppermute | solution.py:407
  31.6 1.5 %collective-permute-start.11 = (f32[4,128]{1,0:T(4,128)S(1)}, f32[4,128]{1,0:T(4,128)S(1)}, u32[]{:S(2)}, u32[]{:S(2)}) collective-permute-start(f32[4,128]{1,0:T(4,128)S(1)} %slice.25), channel_id=1, source_target_pairs={{0,224},{32,192},{64,160},{96,128},{128,96},{160,64},{192,32},{224... | collective-permute-start | bytes 6152 | tf_op jit(solution)/shard_map/ppermute | solution.py:407
  33.0 0.2 collective-permute-start.10
  33.3 0.0 copy-done
  33.3 1.0 %middle.1 = (f32[512,128]{1,0:T(8,128)S(1)}, f32[16,32,128]{2,1,0:T(8,128)S(1)}) custom-call(f32[8,128]{1,0:T(8,128)S(1)} %get-tuple-element.44.scale_ref, f32[44,128]{1,0:T(8,128)S(1)} %pad_add_fusion.alpha_ref, f32[512,512]{1,0:T(8,128)S(1)} %copy-done, f32[512,3072]{1,0:T(8,128)S(1)} %get-tuple-element.77.q_ref, f32[256,160]{1,0:T(8,128)S(1)} %local.2.near_ref, ...), custom_call_target="tpu_custom_call" | custom-call | flops 3670016 | bytes 7000000 | tf_op jit(solution)/shard_map/middle/pallas_call | solution.py:488
  34.3 0.6 %collective-permute-done.12 = f32[4,128]{1,0:T(4,128)S(1)} collective-permute-done((f32[4,128]{1,0:T(4,128)S(1)}, f32[4,128]{1,0:T(4,128)S(1)}, u32[]{:S(2)}, u32[]{:S(2)}) %collective-permute-start.12) | collective-permute-done | bytes 2080 | tf_op jit(solution)/shard_map/ppermute | solution.py:407
  34.9 0.9 %collective-permute-done.11 = f32[4,128]{1,0:T(4,128)S(1)} collective-permute-done((f32[4,128]{1,0:T(4,128)S(1)}, f32[4,128]{1,0:T(4,128)S(1)}, u32[]{:S(2)}, u32[]{:S(2)}) %collective-permute-start.11) | collective-permute-done | bytes 2080 | tf_op jit(solution)/shard_map/ppermute | solution.py:407
  35.8 0.2 collective-permute-done.10
  36.1 1.0 %final.1 = (f32[16,32,128]{2,1,0:T(8,128)}, f32[1,512]{1,0:T(1,128)}) custom-call(f32[8,128]{1,0:T(8,128)S(1)} %get-tuple-element.44.scale_ref, f32[4,128]{1,0:T(4,128)S(1)} %add_add_fusion.alpha_ref, f32[512,128]{1,0:T(8,128)S(1)} %get-tuple-element.82.base_ref, f32[16,32,128]{2,1,0:T(8,128)S(1)} %get-tuple-element.83.local_ref, ...), custom_call_target="tpu_custom_call" | custom-call | flops 524288 | bytes 1500000 | tf_op jit(solution)/shard_map/final/pallas_call | solution.py:498
  (12 shorter events, 0.1 us)
Async XLA Ops:
  3.8 29.4 %copy-start = (f32[512,512]{1,0:T(8,128)S(1)}, f32[512,512]{1,0:T(8,128)}, u32[]{:S(2)}) copy-start(f32[512,512]{1,0:T(8,128)} %leaf_ref.1) | copy-start | bytes 3145732
  3.8 4.2 %collective-permute-start = (f32[32,128]{1,0:T(8,128)S(1)}, f32[32,128]{1,0:T(8,128)S(1)}, u32[]{:S(2)}, u32[]{:S(2)}) collective-permute-start(f32[32,128]{1,0:T(8,128)S(1)} %get-tuple-element.45.face_a_ref), channel_id=1, source_target_pairs={{0,32},{32,0},{64,96},{96,64},{128,160},{160,128},{192,224},{224,1... | collective-permute-start | bytes 49160 | tf_op jit(solution)/shard_map/ppermute | solution.py:407
  7.1 5.6 %collective-permute-start.1 = (f32[4,128]{1,0:T(4,128)S(1)}, f32[4,128]{1,0:T(4,128)S(1)}, u32[]{:S(2)}, u32[]{:S(2)}) collective-permute-start(f32[4,128]{1,0:T(4,128)S(1)} %get-tuple-element.47), channel_id=1, source_target_pairs={{0,224},{32,64},{64,32},{96,128},{128,96},{160,192},{192,160},{224... | collective-permute-start | bytes 6152 | tf_op jit(solution)/shard_map/ppermute | solution.py:411
  8.0 6.4 %collective-permute-start.4 = (f32[36,128]{1,0:T(8,128)S(1)}, f32[36,128]{1,0:T(8,128)S(1)}, u32[]{:S(2)}, u32[]{:S(2)}) collective-permute-start(f32[36,128]{1,0:T(8,128)S(1)} %slice.27), channel_id=1, source_target_pairs={{0,34},{1,35},{2,32},{3,33},{4,38},{5,39},{6,36},{7,37},{8,42},{9,... | collective-permute-start | bytes 55304 | tf_op jit(solution)/shard_map/ppermute | solution.py:442
  11.3 5.1 %collective-permute-start.3 = (f32[36,128]{1,0:T(8,128)S(1)}, f32[36,128]{1,0:T(8,128)S(1)}, u32[]{:S(2)}, u32[]{:S(2)}) collective-permute-start(f32[36,128]{1,0:T(8,128)S(1)} %slice.27), channel_id=1, source_target_pairs={{0,35},{1,34},{2,33},{3,32},{4,39},{5,38},{6,37},{7,36},{8,43},{9,... | collective-permute-start | bytes 55304 | tf_op jit(solution)/shard_map/ppermute | solution.py:442
  12.9 3.6 %collective-permute-start.2 = (f32[84,128]{1,0:T(8,128)S(1)}, f32[84,128]{1,0:T(8,128)S(1)}, u32[]{:S(2)}, u32[]{:S(2)}) collective-permute-start(f32[84,128]{1,0:T(8,128)S(1)} %get-tuple-element.48), channel_id=1, source_target_pairs={{0,1},{1,0},{2,3},{3,2},{4,5},{5,4},{6,7},{7,6},{8,9},{9,8},{10,11... | collective-permute-start | bytes 129032 | tf_op jit(solution)/shard_map/ppermute | solution.py:407
  16.4 7.7 %collective-permute-start.5 = (f32[28,128]{1,0:T(8,128)S(1)}, f32[28,128]{1,0:T(8,128)S(1)}, u32[]{:S(2)}, u32[]{:S(2)}) collective-permute-start(f32[28,128]{1,0:T(8,128)S(1)} %slice.22), channel_id=1, source_target_pairs={{0,38},{1,39},{2,36},{3,37},{4,34},{5,35},{6,32},{7,33},{8,46},{9,... | collective-permute-start | bytes 43016 | tf_op jit(solution)/shard_map/ppermute | solution.py:442
  20.8 7.7 %collective-permute-start.9 = (f32[40,128]{1,0:T(8,128)S(1)}, f32[40,128]{1,0:T(8,128)S(1)}, u32[]{:S(2)}, u32[]{:S(2)}) collective-permute-start(f32[40,128]{1,0:T(8,128)S(1)} %get-tuple-element.75), channel_id=1, source_target_pairs={{0,31},{1,2},{2,1},{3,4},{4,3},{5,6},{6,5},{7,8},{8,7},{9,10},{10,... | collective-permute-start | bytes 61448 | tf_op jit(solution)/shard_map/ppermute | solution.py:411
  24.2 5.8 %collective-permute-start.8 = (f32[12,128]{1,0:T(8,128)S(1)}, f32[12,128]{1,0:T(8,128)S(1)}, u32[]{:S(2)}, u32[]{:S(2)}) collective-permute-start(f32[12,128]{1,0:T(8,128)S(1)} %slice.24), channel_id=1, source_target_pairs={{0,48},{1,49},{2,50},{3,51},{4,52},{5,53},{6,54},{7,55},{8,56},{9,... | collective-permute-start | bytes 18440 | tf_op jit(solution)/shard_map/ppermute | solution.py:442
  26.0 4.3 %collective-permute-start.7 = (f32[12,128]{1,0:T(8,128)S(1)}, f32[12,128]{1,0:T(8,128)S(1)}, u32[]{:S(2)}, u32[]{:S(2)}) collective-permute-start(f32[12,128]{1,0:T(8,128)S(1)} %slice.24), channel_id=1, source_target_pairs={{0,56},{1,57},{2,58},{3,59},{4,60},{5,61},{6,62},{7,63},{8,48},{9,... | collective-permute-start | bytes 18440 | tf_op jit(solution)/shard_map/ppermute | solution.py:442
  26.3 3.9 %collective-permute-start.6 = (f32[20,128]{1,0:T(8,128)S(1)}, f32[20,128]{1,0:T(8,128)S(1)}, u32[]{:S(2)}, u32[]{:S(2)}) collective-permute-start(f32[20,128]{1,0:T(8,128)S(1)} %slice.23), channel_id=1, source_target_pairs={{0,40},{1,41},{2,42},{3,43},{4,44},{5,45},{6,46},{7,47},{8,32},{9,... | collective-permute-start | bytes 30728 | tf_op jit(solution)/shard_map/ppermute | solution.py:442
  30.3 4.6 %collective-permute-start.12 = (f32[4,128]{1,0:T(4,128)S(1)}, f32[4,128]{1,0:T(4,128)S(1)}, u32[]{:S(2)}, u32[]{:S(2)}) collective-permute-start(f32[4,128]{1,0:T(4,128)S(1)} %slice.25), channel_id=1, source_target_pairs={{0,160},{32,128},{64,224},{96,192},{128,32},{160,0},{192,96},{224,... | collective-permute-start | bytes 6152 | tf_op jit(solution)/shard_map/ppermute | solution.py:407
  31.6 4.3 %collective-permute-start.11 = (f32[4,128]{1,0:T(4,128)S(1)}, f32[4,128]{1,0:T(4,128)S(1)}, u32[]{:S(2)}, u32[]{:S(2)}) collective-permute-start(f32[4,128]{1,0:T(4,128)S(1)} %slice.25), channel_id=1, source_target_pairs={{0,224},{32,192},{64,160},{96,128},{128,96},{160,64},{192,32},{224... | collective-permute-start | bytes 6152 | tf_op jit(solution)/shard_map/ppermute | solution.py:407
  33.0 3.0 %collective-permute-start.10 = (f32[4,128]{1,0:T(4,128)S(1)}, f32[4,128]{1,0:T(4,128)S(1)}, u32[]{:S(2)}, u32[]{:S(2)}) collective-permute-start(f32[4,128]{1,0:T(4,128)S(1)} %slice.25), channel_id=1, source_target_pairs={{0,96},{32,64},{64,32},{96,0},{128,224},{160,192},{192,160},{224,1... | collective-permute-start | bytes 6152 | tf_op jit(solution)/shard_map/ppermute | solution.py:407
